TPU v7x, 128 devices: a whole 4x4x4 slice. The times are simulated.
128 devices in a mesh: seq: 8 (over z, x_hi), fsdp: 16 (over x_lo, y, core).
Axes of the slice: x: 4 (x_hi: 2, x_lo: 2; x = x_hi * 2 + x_lo), y: 4, z: 4, core: 2. Of those that a mesh axis runs over, the one named last changes fastest.
Arguments:
- middle_state: bfloat16 [16, 4096, 4096], P('fsdp', 'seq'), may hold values from -80 to 80
- newest_state: bfloat16 [16, 4096, 4096], P('fsdp', 'seq'), may hold values from -6 to 6
- middle_cotangent: bfloat16 [16, 4096, 4096], P('fsdp', 'seq'), may hold values from -6 to 6
- newest_cotangent: bfloat16 [16, 4096, 4096], P('fsdp', 'seq'), may hold values from -6 to 6
- log_decay: int32 [16, 4096, 32], P('fsdp', 'seq'), may hold values from -3079 to 0
- state_weights: bfloat16 [4096, 256], P('fsdp'), may hold values from -0.09375 to 0.09375
- skip_gain: float32 [32], replicated, may hold values from 0.5 to 1.5
Outputs:
- rebuilt_oldest: bfloat16 [16, 4096, 4096], P('fsdp', 'seq')
- middle_gradient: bfloat16 [16, 4096, 4096], P('fsdp', 'seq')
- weights_gradient: float32 [4096, 256], P(('seq', 'fsdp'))
All inputs are finite; a program needn't handle non-finite values.
Results may differ from a plain program's by a relative error of at most 0.017.
Values may be sent and summed in bfloat16 or wider, within the bound.
A program may use at most 256 MiB of HBM per device.

v0:
```python
import jax
import jax.numpy as jnp
from jax import lax
from jax.sharding import PartitionSpec as P

HALF_HEADS = 32
P_SIZE = 128
N = 128
GROUP = 256


norm_epsilon = 1e-05
decay_unit = 1.0 / 4096.0


def carried_in(x, axis, join, neutral, backward):
    count = lax.axis_size(axis)
    place = lax.axis_index(axis)
    ahead = count - 1 - place if backward else place
    gathered = jax.tree.map(
        lambda a, kind: lax.all_gather(a.astype(kind), axis), x, (jnp.bfloat16, jnp.bfloat16)
    )
    state = jax.tree.map(lambda a, e: jnp.zeros_like(a) + jnp.asarray(e, a.dtype), x, neutral)

    def one(hop, state):
        source = count - 1 - hop if backward else hop
        return join(
            state,
            jax.tree.map(
                lambda a, own: lax.dynamic_index_in_dim(a, source, 0, False).astype(own.dtype),
                gathered,
                x,
            ),
        )

    return lax.fori_loop(0, ahead, one, state)


def split_up(x, dim, peers):
    before, after = (x.shape[:dim], x.shape[dim + 1 :])
    return jnp.moveaxis(x.reshape(*before, peers, -1, *after), dim, 0)


def sum_at_owner(x, axis, dim):
    peers = lax.axis_size(axis)
    parts = lax.all_to_all(split_up(x, dim, peers), axis, 0, 0, tiled=True)
    return jnp.sum(parts.astype(jnp.float32), axis=0)


def normalize(values):
    return values * lax.rsqrt(jnp.mean(values * values, axis=-1, keepdims=True) + norm_epsilon)


def group_pass(state_now, pieces, skip_gain):
    features, entry_key, readout, log_rates = pieces
    length = log_rates.shape[0]
    running = jnp.cumsum(log_rates, axis=0)
    input_feed = jnp.sqrt(1.0 - jnp.exp(2.0 * log_rates))
    inputs = features * input_feed[:, :, None]
    scores = jnp.dot(readout, entry_key.T)
    later_index = lax.broadcasted_iota(jnp.int32, (length, length), 0)
    earlier_index = lax.broadcasted_iota(jnp.int32, (length, length), 1)
    causal = (later_index >= earlier_index)[None]
    heads_first = running.T
    log_gaps = heads_first[:, :, None] - heads_first[:, None, :]
    mix_weights = jnp.where(causal, jnp.exp(jnp.where(causal, log_gaps, 0.0)), 0.0) * scores[None]
    within = jnp.einsum("hts,shp->thp", mix_weights, inputs)
    carried = jnp.einsum("tn,hpn->thp", readout, state_now) * jnp.exp(running)[:, :, None]
    outputs = (within + carried) * N ** (-0.5) + skip_gain[None, :, None] * features
    tail_decay = jnp.exp(running[-1][None, :] - running)
    new_state = state_now * jnp.exp(running[-1])[:, None, None] + jnp.einsum(
        "shp,sn->hpn", inputs * tail_decay[:, :, None], entry_key
    )
    return (new_state, outputs)


def run_rows(feature_values, projected_values, log_rates, skip_gain, start_state):
    row_count = feature_values.shape[0]
    block_count = row_count // GROUP
    features = feature_values.reshape(block_count, GROUP, HALF_HEADS, P_SIZE)
    entry_key = projected_values[:, :N].reshape(block_count, GROUP, N)
    readout = projected_values[:, N:].reshape(block_count, GROUP, N)
    log_blocks = log_rates.reshape(block_count, GROUP, HALF_HEADS)

    def step_block(state_now, pieces):
        return group_pass(state_now, pieces, skip_gain)

    final_state, outputs = lax.scan(
        step_block, start_state, (features, entry_key, readout, log_blocks)
    )
    return (outputs.reshape(row_count, HALF_HEADS * P_SIZE), final_state)


def combine_decay(earlier, later):
    return (earlier[0] * later[0], later[0][:, None, None] * earlier[1] + later[1])


def shards(
    middle_state,
    newest_state,
    middle_cotangent,
    newest_cotangent,
    log_decay,
    state_weights,
    skip_gain,
):
    row_count = middle_state.shape[1]
    seq_devices = lax.axis_size("seq")
    fsdp_devices = lax.axis_size("fsdp")
    normed, norm_back = jax.vjp(normalize, middle_state[0].astype(jnp.float32))
    features = normed.astype(jnp.bfloat16)
    weights_full = lax.all_gather(state_weights, "fsdp", axis=0, tiled=True)
    projected = jnp.dot(features, weights_full, preferred_element_type=jnp.float32).astype(
        jnp.bfloat16
    )
    log_rates = log_decay[0].astype(jnp.float32) * decay_unit
    features_float = features.astype(jnp.float32)
    projected_float = projected.astype(jnp.float32)
    running = jnp.cumsum(log_rates, axis=0)
    total_log = running[-1]
    decay_all = jnp.exp(total_log)
    input_feed = jnp.sqrt(1.0 - jnp.exp(2.0 * log_rates))
    tail_decay = jnp.exp(total_log[None, :] - running)
    heads_view = features_float.reshape(row_count, HALF_HEADS, P_SIZE)
    local_state = jnp.einsum(
        "shp,sn->hpn", heads_view * (input_feed * tail_decay)[:, :, None], projected_float[:, :N]
    )
    identity = (
        jnp.ones((HALF_HEADS,), jnp.float32),
        jnp.zeros((HALF_HEADS, P_SIZE, N), jnp.float32),
    )
    unused_decay, state_in = carried_in(
        (decay_all, local_state), "seq", combine_decay, identity, False
    )

    def local_mix(feature_values, projected_values):
        return run_rows(feature_values, projected_values, log_rates, skip_gain, state_in)

    (mixed_out, final_state), mix_back = jax.vjp(local_mix, features_float, projected_float)
    rebuilt = (newest_state[0].astype(jnp.float32) - mixed_out).astype(jnp.bfloat16)
    upstream = newest_cotangent[0].astype(jnp.float32)
    leading = jnp.exp(running)
    back_local = jnp.einsum(
        "thp,tn->hpn",
        upstream.reshape(row_count, HALF_HEADS, P_SIZE) * leading[:, :, None],
        projected_float[:, N:],
    ) * N ** (-0.5)
    unused_back, state_grad = carried_in(
        (decay_all, back_local), "seq", combine_decay, identity, True
    )
    feature_grad, projected_grad = mix_back((upstream, state_grad))
    projected_low = projected_grad.astype(jnp.bfloat16)
    through_weights = lax.dot_general(
        projected_low, weights_full, (((1,), (1,)), ((), ())), preferred_element_type=jnp.float32
    )
    (norm_grad,) = norm_back(feature_grad + through_weights)
    gradient_out = (middle_cotangent[0].astype(jnp.float32) + norm_grad).astype(jnp.bfloat16)
    halfway = lax.psum_scatter(
        lax.dot_general(
            features, projected_low, (((0,), (0,)), ((), ())), preferred_element_type=jnp.float32
        ).astype(jnp.bfloat16),
        "seq",
        scatter_dimension=0,
        tiled=True,
    )
    summed = sum_at_owner(halfway, "fsdp", 0)
    factor_scale = (row_count * seq_devices * fsdp_devices) ** (-0.5)
    return (rebuilt[None], gradient_out[None], summed * factor_scale)


def solution(mesh):
    return jax.shard_map(
        shards,
        mesh=mesh,
        in_specs=(
            P("fsdp", "seq", None),
            P("fsdp", "seq", None),
            P("fsdp", "seq", None),
            P("fsdp", "seq", None),
            P("fsdp", "seq", None),
            P("fsdp", None),
            P(),
        ),
        out_specs=(P("fsdp", "seq", None), P("fsdp", "seq", None), P(("seq", "fsdp"), None)),
        check_vma=False,
    )
```

profile of v0, /device:TPU:0, one launch (start us, length us, event | category | flops | bytes accessed | tf_op | source)
XLA Modules:
  0.0 452.5 jit_solution(10677422256003471732)
XLA Ops:
  8.8 1.2 reduce-window.24
  10.2 7.1 %copy.95 = f32[1,512,4096]{1,2,0:T(8,128)} copy(bf16[1,512,4096]{2,1,0:T(8,128)(2,1)} %param.15) | data formatting | bytes 12582912 | tf_op jit(solution)/shard_map/convert_element_type | solution.py:110
  17.6 3.1 fusion.121
  21.2 24.9 %all-gather.7.cloned.1.call-done = bf16[4096,256]{1,0:T(8,128)(2,1)} async-done(((bf16[256,256]{1,0:T(8,128)(2,1)}), bf16[4096,256]{1,0:T(8,128)(2,1)}) %all-gather.7.cloned.1.call-update) | async-done | bytes 2097168 | tf_op jit(solution)/shard_map/all_gather | solution.py:112
  46.1 4.3 fusion.142
  51.4 2.2 fusion.139
  53.7 7.1 %copy.96 = f32[1,512,4096]{1,2,0:T(8,128)} copy(bf16[1,512,4096]{2,1,0:T(8,128)(2,1)} %param.18) | data formatting | bytes 12582912 | tf_op jit(solution)/shard_map/convert_element_type | solution.py:141
  60.8 6.0 %multiply_convert_fusion.3 = bf16[32,128,128]{2,1,0:T(8,128)(2,1)} fusion(f32[512,32,128]{0,2,1:T(8,128)} %bitcast.420, f32[512,32]{0,1:T(8,128)S(1)} %get-tuple-element.1096, bf16[512,256]{1,0:T(8,128)(2,1)S(1)} %fusion.142), kind=kOutput, calls=%fused_computation.170 | convolution fusion | flops 540016640 | bytes 9633792 | tf_op jit(solution)/shard_map/thp,tn->hpn/dot_general | solution.py:143
  67.2 23.2 %all-gather.2 = bf16[8,1,32]{2,1,0:T(2,128)(2,1)S(1)} all-gather(bf16[1,1,32]{2,1,0:T(2,128)(2,1)S(1)} %bitcast.437), channel_id=1, replica_groups=mesh['seq'=8,'fsdp'=16] {'seq'}, dimensions={0}, use_global_device_ids=true | all-gather | bytes 576 | tf_op jit(solution)/shard_map/all_gather | solution.py:21
  90.4 3.3 convert_bitcast_fusion
  93.7 5.7 %copy.118 = f32[64,8,32,128]{3,2,1,0:T(8,128)} copy(f32[64,8,32,128]{3,1,2,0:T(8,128)S(1)} %convert_bitcast_fusion) | data formatting | bytes 16777216
  99.4 9.9 %copy.81 = f32[2,256,32,128]{1,3,2,0:T(8,128)} copy(f32[2,256,32,128]{3,2,1,0:T(8,128)} %bitcast.422) | data formatting | bytes 16777216 | tf_op jit(solution)/shard_map/convert_element_type | solution.py:110
  109.4 3.3 convert_bitcast_fusion.1
  112.6 5.0 %copy.119 = f32[64,8,32,128]{3,2,1,0:T(8,128)} copy(f32[64,8,32,128]{3,1,2,0:T(8,128)S(1)} %convert_bitcast_fusion.1) | data formatting | bytes 16777216
  117.7 7.7 %fusion.129 = f32[2,256,32,128]{1,3,2,0:T(8,128)} fusion(f32[2,256,32,128]{1,3,2,0:T(8,128)} %copy.81, f32[2,256]{1,0:T(2,128)S(1)} %rsqrt.15), kind=kLoop, calls=%fused_computation.164 | loop fusion | flops 6291456 | bytes 16779264 | tf_op jit(solution)/shard_map/convert_element_type | solution.py:117
  125.4 35.7 %all-gather.9.cloned.1.call-done = bf16[256,128,128]{2,1,0:T(8,128)(2,1)} async-done(((bf16[32,128,128]{2,1,0:T(8,128)(2,1)}), bf16[256,128,128]{2,1,0:T(8,128)(2,1)}) %all-gather.9.cloned.1.call-update) | async-done | bytes 8388624 | tf_op jit(solution)/shard_map/all_gather | solution.py:21
  161.9 4.3 broadcast.241.clone2
  166.2 66.1 %while.85 = (s32[]{:T(128)}, f32[32,128,128]{2,1,0:T(8,128)S(1)}, f32[2,256,32,128]{3,2,1,0:T(8,128)}, f32[2,256,32,1]{1,2,3,0:T(8,128)S(1)}, bf16[2,128,256]{1,...) while((s32[]{:T(128)}, f32[32,128,128]{2,1,0:T(8,128)S(1)}, ...), condition=%wide.region_8.9_spmd.clone.clone, body=%wide.region_5.8_spmd.clone.clone.sunk | while | flops 1119936640 | bytes 218278640 | solution.py:88
  167.3 6.7 %multiply_dynamic-update-slice_fusion.5 = (bf16[2,32,256,256]{3,2,1,0:T(8,128)(2,1)}, f32[2,32,256,256]{3,2,1,0:T(8,128)}) fusion(bf16[2,32,256,256]{3,2,1,0:T(8,128)(2,1)} %get-tuple-element.1475, s32[]{:T(128)} %get-tuple-element.1469, f32[256,256]{1,0:T(8,128)S(1)} %fusion.226, f32[32,256]{1,0:T(8,128)S(1)} %get-tuple-element.1415, ...), kind=kLoop, calls=%fused_computation.75.clone.1 | loop fusion | flops 8388608 | bytes 17170944 | tf_op jit(solution)/shard_map/jvp()/while/body/jit(dynamic_update_index_in_dim)/dynamic_update_slice | solution.py:88
  174.5 2.4 fusion.227
  177.0 2.9 fusion.228
  179.9 5.5 %copy.195 = f32[1,256,32,128]{3,2,1,0:T(8,128)} copy(f32[1,256,32,128]{1,3,2,0:T(8,128)} %fusion.228) | data formatting | bytes 8388608 | tf_op jit(solution)/shard_map/jvp()/while/body/jit(dynamic_update_index_in_dim)/dynamic_update_slice | solution.py:88
  185.4 4.9 %constant_dynamic-update-slice_fusion.4 = f32[2,256,32,128]{3,2,1,0:T(8,128)} fusion(f32[2,256,32,128]{3,2,1,0:T(8,128)} %get-tuple-element.1471, f32[1,256,32,128]{3,2,1,0:T(8,128)} %copy.195, s32[]{:T(128)} %get-tuple-element.1469), kind=kLoop, calls=%fused_computation.135.clone.1 | loop fusion | bytes 8389120 | tf_op jit(solution)/shard_map/jvp()/while/body/jit(dynamic_update_index_in_dim)/dynamic_update_slice | solution.py:88
  191.8 3.5 multiply_dynamic-update-slice_fusion.6
  196.3 1.1 multiply_add_fusion.6
  197.5 1.2 copy-done.6
  200.5 6.6 %multiply_dynamic-update-slice_fusion.5 = (bf16[2,32,256,256]{3,2,1,0:T(8,128)(2,1)}, f32[2,32,256,256]{3,2,1,0:T(8,128)}) fusion(bf16[2,32,256,256]{3,2,1,0:T(8,128)(2,1)} %get-tuple-element.1475, s32[]{:T(128)} %get-tuple-element.1469, f32[256,256]{1,0:T(8,128)S(1)} %fusion.226, f32[32,256]{1,0:T(8,128)S(1)} %get-tuple-element.1415, ...), kind=kLoop, calls=%fused_computation.75.clone.1 | loop fusion | flops 8388608 | bytes 17170944 | tf_op jit(solution)/shard_map/jvp()/while/body/jit(dynamic_update_index_in_dim)/dynamic_update_slice | solution.py:88
  207.6 2.4 fusion.227
  210.1 2.9 fusion.228
  213.0 5.5 %copy.195 = f32[1,256,32,128]{3,2,1,0:T(8,128)} copy(f32[1,256,32,128]{1,3,2,0:T(8,128)} %fusion.228) | data formatting | bytes 8388608 | tf_op jit(solution)/shard_map/jvp()/while/body/jit(dynamic_update_index_in_dim)/dynamic_update_slice | solution.py:88
  218.5 5.0 %constant_dynamic-update-slice_fusion.4 = f32[2,256,32,128]{3,2,1,0:T(8,128)} fusion(f32[2,256,32,128]{3,2,1,0:T(8,128)} %get-tuple-element.1471, f32[1,256,32,128]{3,2,1,0:T(8,128)} %copy.195, s32[]{:T(128)} %get-tuple-element.1469), kind=kLoop, calls=%fused_computation.135.clone.1 | loop fusion | bytes 8389120 | tf_op jit(solution)/shard_map/jvp()/while/body/jit(dynamic_update_index_in_dim)/dynamic_update_slice | solution.py:88
  224.8 3.4 multiply_dynamic-update-slice_fusion.6
  229.2 1.2 multiply_add_fusion.6
  230.4 1.2 copy-done.6
  232.3 36.3 %all-gather.11.cloned.1.call-done = bf16[256,128,128]{2,1,0:T(8,128)(2,1)} async-done(((bf16[32,128,128]{2,1,0:T(8,128)(2,1)}), bf16[256,128,128]{2,1,0:T(8,128)(2,1)}) %all-gather.11.cloned.1.call-update) | async-done | bytes 8388624 | tf_op jit(solution)/shard_map/all_gather | solution.py:21
  268.8 11.9 %while.83 = (s32[]{:T(128)}, f32[32,128,128]{2,1,0:T(8,128)S(1)}, s32[]{:T(128)}, bf16[8,32]{1,0:T(8,128)(2,1)S(1)}, bf16[8,32,128,128]{3,2,1,0:T(8,128)(2,1)}, ...) while((s32[]{:T(128)}, f32[32,128,128]{2,1,0:T(8,128)S(1)}, s32[]{:T(128)}, bf16[8,32]{1,0:T(8,128)(2,1)S(1)}, ...), condition=%wide.region_10.11_spmd, body=%wide.region_9.10_spmd.sunk | while | flops 1572902 | bytes 5243347 | solution.py:36
  268.8 1.7 convert_add_fusion.5
  270.5 1.7 convert_add_fusion.5
  272.2 1.7 convert_add_fusion.5
  273.9 1.7 convert_add_fusion.5
  275.6 1.7 convert_add_fusion.5
  277.3 1.7 convert_add_fusion.5
  279.0 1.7 convert_add_fusion.5
  280.7 4.3 broadcast.241.clone
  285.1 70.6 %while.84 = (s32[]{:T(128)}, f32[32,128,128]{2,1,0:T(8,128)S(1)}, f32[2,256,32,128]{3,2,1,0:T(8,128)}, f32[2,256,128]{2,1,0:T(8,128)S(1)}, f32[2,256,128]{2,1,0:...) while((s32[]{:T(128)}, f32[32,128,128]{2,1,0:T(8,128)S(1)}, ...), condition=%wide.region_13.14_spmd, body=%wide.region_11.13_spmd.sunk | while | flops 2195726336 | bytes 120263224 | solution.py:88
  285.2 2.6 constant_dynamic-slice_fusion.5
  288.6 10.7 %fusion.212 = f32[1,256,32,128]{3,1,2,0:T(8,128)S(1)} fusion(f32[256,32,128]{2,0,1:T(8,128)S(1)} %fusion.211, f32[1,256,32,128]{3,2,1,0:T(8,128)S(1)} %constant_dynamic-slice_fusion.5, bf16[2,32,256,256]{3,2,1,0:T(8,128)(2,1)} %get-tuple-element.1590, s32[]{:T(128)S(6)} %sub.203, f32[256,32]{0,1:T(8,128)S(1)} %get-tuple-element.1391, ...), kind=kOutput, calls=%fused_computation.18.clone.1 | convolution fusion | flops 543162368 | bytes 21037572 | tf_op jit(solution)/shard_map/transpose(jvp())/while/body/eval_jaxpr/hts,shp->thp/dot_general | solution.py:67
  299.4 4.4 copy_dynamic-update-slice_fusion.2
  303.7 2.8 fusion.216
  306.6 7.1 %fusion.214 = bf16[256,256]{1,0:T(8,128)(2,1)S(1)} fusion(f32[2,32,256,256]{3,2,1,0:T(8,128)} %get-tuple-element.1593, s32[]{:T(128)S(6)} %sub.203, bf16[2,256,32,128]{1,3,2,0:T(8,128)(2,1)S(1)} %copy-done.7, f32[1,256,32,128]{3,2,1,0:T(8,128)S(1)} %constant_dynamic-slice_fusion.5), kind=kOutput, calls=%fused_computation.6.clone.1 | convolution fusion | flops 542048256 | bytes 14812160 | tf_op jit(solution)/shard_map/transpose(jvp())/while/body/eval_jaxpr/hts,shp->thp/dot_general | solution.py:67
  314.7 5.4 %multiply_add_fusion.5 = f32[32,128,128]{2,1,0:T(8,128)S(1)} fusion(f32[32,128,128]{2,1,0:T(8,128)S(1)} %get-tuple-element.1559, f32[1,256,32,128]{3,2,1,0:T(8,128)S(1)} %constant_dynamic-slice_fusion.5, f32[256,32]{0,1:T(8,128)S(1)} %multiply_bitcast_fusion.2, f32[32]{0:T(128)S(1)} %fusion.210, bf16[2,256,128]{2,1,0:T(8,128)(2,1)S(1)} %get-tuple-element.1586, ...), kind=kOutput, calls=%fused_computation.41.clone.1 | convolution fusion | flops 270532608 | bytes 8487428 | tf_op jit(solution)/shard_map/transpose(jvp())/while/body/eval_jaxpr/tn,hpn->thp/dot_general | solution.py:68
  320.3 2.6 constant_dynamic-slice_fusion.5
  323.7 10.7 %fusion.212 = f32[1,256,32,128]{3,1,2,0:T(8,128)S(1)} fusion(f32[256,32,128]{2,0,1:T(8,128)S(1)} %fusion.211, f32[1,256,32,128]{3,2,1,0:T(8,128)S(1)} %constant_dynamic-slice_fusion.5, bf16[2,32,256,256]{3,2,1,0:T(8,128)(2,1)} %get-tuple-element.1590, s32[]{:T(128)S(6)} %sub.203, f32[256,32]{0,1:T(8,128)S(1)} %get-tuple-element.1391, ...), kind=kOutput, calls=%fused_computation.18.clone.1 | convolution fusion | flops 543162368 | bytes 21037572 | tf_op jit(solution)/shard_map/transpose(jvp())/while/body/eval_jaxpr/hts,shp->thp/dot_general | solution.py:67
  334.4 4.4 copy_dynamic-update-slice_fusion.2
  338.9 2.8 fusion.216
  341.7 7.1 %fusion.214 = bf16[256,256]{1,0:T(8,128)(2,1)S(1)} fusion(f32[2,32,256,256]{3,2,1,0:T(8,128)} %get-tuple-element.1593, s32[]{:T(128)S(6)} %sub.203, bf16[2,256,32,128]{1,3,2,0:T(8,128)(2,1)S(1)} %copy-done.7, f32[1,256,32,128]{3,2,1,0:T(8,128)S(1)} %constant_dynamic-slice_fusion.5), kind=kOutput, calls=%fused_computation.6.clone.1 | convolution fusion | flops 542048256 | bytes 14812160 | tf_op jit(solution)/shard_map/transpose(jvp())/while/body/eval_jaxpr/hts,shp->thp/dot_general | solution.py:67
  349.8 5.4 %multiply_add_fusion.5 = f32[32,128,128]{2,1,0:T(8,128)S(1)} fusion(f32[32,128,128]{2,1,0:T(8,128)S(1)} %get-tuple-element.1559, f32[1,256,32,128]{3,2,1,0:T(8,128)S(1)} %constant_dynamic-slice_fusion.5, f32[256,32]{0,1:T(8,128)S(1)} %multiply_bitcast_fusion.2, f32[32]{0:T(128)S(1)} %fusion.210, bf16[2,256,128]{2,1,0:T(8,128)(2,1)S(1)} %get-tuple-element.1586, ...), kind=kOutput, calls=%fused_computation.41.clone.1 | convolution fusion | flops 270532608 | bytes 8487428 | tf_op jit(solution)/shard_map/transpose(jvp())/while/body/eval_jaxpr/tn,hpn->thp/dot_general | solution.py:68
  355.7 5.4 %convolution_convert_fusion = bf16[4096,256]{1,0:T(8,128)(2,1)} fusion(bf16[1,512,4096]{2,1,0:T(8,128)(2,1)} %param.15, f32[512]{0:T(512)S(1)} %copy-done.16, f32[512,128]{1,0:T(8,128)S(1)} %bitcast.427, f32[512,128]{1,0:T(8,128)S(1)} %bitcast.429), kind=kOutput, calls=%fused_computation.163 | convolution fusion | flops 1081344000 | bytes 6817792 | tf_op jit(solution)/shard_map/dot_general | solution.py:159
  361.1 9.6 %reshape.318 = f32[1,512,4096]{2,1,0:T(8,128)} reshape(f32[2,256,32,128]{3,2,1,0:T(8,128)} %get-tuple-element.732) | data formatting | bytes 16777216 | tf_op jit(solution)/shard_map/jvp()/reshape | solution.py:91
  370.7 10.3 %fusion.123 = (f32[512]{0:T(512)S(1)}, f32[512,4096]{1,0:T(8,128)S(1)}) fusion(bf16[1,512,4096]{2,1,0:T(8,128)(2,1)} %param.15, bf16[4096,256]{1,0:T(8,128)(2,1)S(1)} %copy-done.12, f32[512,128]{1,0:T(8,128)S(1)} %bitcast.428, f32[512,128]{1,0:T(8,128)S(1)} %bitcast.430, f32[64,8,32,128]{3,2,1,0:T(8,128)} %bitcast.419), kind=kOutput, calls=%fused_computation.154 | convolution fusion | flops 1082392064 | bytes 23595008 | tf_op jit(solution)/shard_map/dot_general | solution.py:153
  381.0 4.4 fusion.130
  385.4 47.2 %reduce-scatter.2.cloned.1.call-done = bf16[512,256]{1,0:T(8,128)(2,1)} async-done(((bf16[4096,256]{1,0:T(8,128)(2,1)}), bf16[512,256]{1,0:T(8,128)(2,1)}) %reduce-scatter.2.cloned.1.call-update) | async-done | bytes 262160 | tf_op jit(solution)/shard_map/reduce_scatter | solution.py:158
  432.6 4.4 all-to-all-start
  437.1 8.0 %subtract_convert_fusion = bf16[1,512,4096]{2,1,0:T(8,128)(2,1)} fusion(f32[1,512,4096]{2,1,0:T(8,128)} %reshape.318, bf16[1,512,4096]{2,1,0:T(8,128)(2,1)} %param.16), kind=kLoop, calls=%fused_computation.157 | loop fusion | flops 6291456 | bytes 16777216 | tf_op jit(solution)/shard_map/convert_element_type | solution.py:140
  (169 shorter events, 19.0 us)
Async XLA Ops:
  7.2 38.9 %all-gather.7.cloned.1.call-start = ((), (), s32[]{:S(2)}) async-start(), calls=%async_computation.2 | async-start | bytes 2228224 | tf_op jit(solution)/shard_map/all_gather | solution.py:112
  7.9 153.2 %all-gather.9.cloned.1.call-start = ((), (), s32[]{:S(2)}) async-start(), calls=%async_computation.4 | async-start | bytes 9437184 | tf_op jit(solution)/shard_map/all_gather | solution.py:21
  17.3 3.4 copy-start.13
  20.7 0.6 copy-start.17
  20.7 46.2 %copy-start.15 = (f32[512]{0:T(512)}, f32[512]{0:T(512)S(1)}, u32[]{:S(2)}) copy-start(f32[512]{0:T(512)S(1)} %fusion.146) | copy-start | bytes 6148
  46.1 5.2 %copy-start.1 = (f32[1,512,4096]{1,2,0:T(8,128)S(1)}, f32[1,512,4096]{1,2,0:T(8,128)}, u32[]{:S(2)}) copy-start(f32[1,512,4096]{1,2,0:T(8,128)} %copy.95) | copy-start | bytes 25165828
  53.6 214.9 %all-gather.11.cloned.1.call-start = ((), (), s32[]{:S(2)}) async-start(), calls=%async_computation.5 | async-start | bytes 9437184 | tf_op jit(solution)/shard_map/all_gather | solution.py:21
  66.9 365.8 %reduce-scatter.2.cloned.1.call-start = ((), (), s32[]{:S(2)}) async-start(), calls=%async_computation.3 | async-start | bytes 2359296 | tf_op jit(solution)/shard_map/reduce_scatter | solution.py:158
  161.9 4.3 copy-start.14
  167.1 6.9 %slice-start = ((s8[8388608]{0:T(1024)(128)(4,1)}), s8[4194304]{0:T(1024)(128)(4,1)S(1)}, s32[]{:S(2)}) async-start(s8[8388608]{0:T(1024)(128)(4,1)} %bitcast.414), calls=%async_computation.6 | async-start | bytes 8388608 | tf_op jit(solution)/shard_map/jvp()/while
  167.3 7.2 %slice-start.1 = ((s8[8388608]{0:T(1024)(128)(4,1)}), s8[4194304]{0:T(1024)(128)(4,1)S(1)}, s32[]{:S(2)}) async-start(s8[8388608]{0:T(1024)(128)(4,1)} %bitcast.414), calls=%async_computation.7 | async-start | bytes 8388608 | tf_op jit(solution)/shard_map/jvp()/while
  185.4 5.2 %copy-start.2 = (bf16[2,256,32,128]{1,3,2,0:T(8,128)(2,1)S(1)}, bf16[2,256,32,128]{1,3,2,0:T(8,128)(2,1)}, u32[]{:S(2)}) copy-start(bf16[2,256,32,128]{1,3,2,0:T(8,128)(2,1)} %get-tuple-element.1481) | copy-start | bytes 12582916 | tf_op jit(solution)/shard_map/jvp()/while
  185.4 6.4 %copy-start.5 = (bf16[2,256,32,128]{1,3,2,0:T(8,128)(2,1)S(1)}, bf16[2,256,32,128]{1,3,2,0:T(8,128)(2,1)}, u32[]{:S(2)}) copy-start(bf16[2,256,32,128]{1,3,2,0:T(8,128)(2,1)} %get-tuple-element.1476) | copy-start | bytes 12582916 | tf_op jit(solution)/shard_map/jvp()/while
  190.6 5.0 %slice-start.2 = ((s8[8388608]{0:T(1024)(128)(4,1)}), s8[4194304]{0:T(1024)(128)(4,1)S(1)}, s32[]{:S(2)}) async-start(s8[8388608]{0:T(1024)(128)(4,1)} %bitcast.416), calls=%async_computation.8 | async-start | bytes 8388608 | tf_op jit(solution)/shard_map/jvp()/while
  191.8 3.5 copy-start.8
  191.8 4.5 slice-start.3
  195.3 2.2 copy-start.3
  195.3 3.4 copy-start.6
  196.3 3.0 copy-start.9
  200.3 6.9 %slice-start = ((s8[8388608]{0:T(1024)(128)(4,1)}), s8[4194304]{0:T(1024)(128)(4,1)S(1)}, s32[]{:S(2)}) async-start(s8[8388608]{0:T(1024)(128)(4,1)} %bitcast.414), calls=%async_computation.6 | async-start | bytes 8388608 | tf_op jit(solution)/shard_map/jvp()/while
  200.5 7.1 %slice-start.1 = ((s8[8388608]{0:T(1024)(128)(4,1)}), s8[4194304]{0:T(1024)(128)(4,1)S(1)}, s32[]{:S(2)}) async-start(s8[8388608]{0:T(1024)(128)(4,1)} %bitcast.414), calls=%async_computation.7 | async-start | bytes 8388608 | tf_op jit(solution)/shard_map/jvp()/while
  218.4 5.3 %copy-start.2 = (bf16[2,256,32,128]{1,3,2,0:T(8,128)(2,1)S(1)}, bf16[2,256,32,128]{1,3,2,0:T(8,128)(2,1)}, u32[]{:S(2)}) copy-start(bf16[2,256,32,128]{1,3,2,0:T(8,128)(2,1)} %get-tuple-element.1481) | copy-start | bytes 12582916 | tf_op jit(solution)/shard_map/jvp()/while
  218.4 6.3 %copy-start.5 = (bf16[2,256,32,128]{1,3,2,0:T(8,128)(2,1)S(1)}, bf16[2,256,32,128]{1,3,2,0:T(8,128)(2,1)}, u32[]{:S(2)}) copy-start(bf16[2,256,32,128]{1,3,2,0:T(8,128)(2,1)} %get-tuple-element.1476) | copy-start | bytes 12582916 | tf_op jit(solution)/shard_map/jvp()/while
  223.7 4.8 %slice-start.2 = ((s8[8388608]{0:T(1024)(128)(4,1)}), s8[4194304]{0:T(1024)(128)(4,1)S(1)}, s32[]{:S(2)}) async-start(s8[8388608]{0:T(1024)(128)(4,1)} %bitcast.416), calls=%async_computation.8 | async-start | bytes 8388608 | tf_op jit(solution)/shard_map/jvp()/while
  224.8 3.5 copy-start.8
  224.8 4.4 slice-start.3
  228.2 2.2 copy-start.3
  228.2 3.4 copy-start.6
  229.2 3.0 copy-start.9
  285.1 70.6 %copy-start.16 = (f32[512]{0:T(512)S(1)}, f32[512]{0:T(512)}, u32[]{:S(2)}) copy-start(f32[512]{0:T(512)} %copy-done.15) | copy-start | bytes 6148
  299.4 4.4 copy-start.10
  303.7 2.8 copy-start.7
  306.6 7.3 %copy-start.4 = (bf16[2,256,32,128]{1,3,2,0:T(8,128)(2,1)S(1)}, bf16[2,256,32,128]{1,3,2,0:T(8,128)(2,1)}, u32[]{:S(2)}) copy-start(bf16[2,256,32,128]{1,3,2,0:T(8,128)(2,1)} %get-tuple-element.1592) | copy-start | bytes 12582916 | tf_op jit(solution)/shard_map/transpose(jvp())/while
  334.4 4.4 copy-start.10
  338.8 2.8 copy-start.7
  341.7 7.3 %copy-start.4 = (bf16[2,256,32,128]{1,3,2,0:T(8,128)(2,1)S(1)}, bf16[2,256,32,128]{1,3,2,0:T(8,128)(2,1)}, u32[]{:S(2)}) copy-start(bf16[2,256,32,128]{1,3,2,0:T(8,128)(2,1)} %get-tuple-element.1592) | copy-start | bytes 12582916 | tf_op jit(solution)/shard_map/transpose(jvp())/while
  361.1 9.6 %copy-start.12 = (bf16[4096,256]{1,0:T(8,128)(2,1)S(1)}, bf16[4096,256]{1,0:T(8,128)(2,1)}, u32[]{:S(2)}) copy-start(bf16[4096,256]{1,0:T(8,128)(2,1)} %all-gather.7.cloned.1.call-done) | copy-start | bytes 6291460
  370.6 10.3 %copy-start.18 = (f32[512]{0:T(512)S(1)}, f32[512]{0:T(512)}, u32[]{:S(2)}) copy-start(f32[512]{0:T(512)} %copy-done.17) | copy-start | bytes 6148
  370.6 10.3 %copy-start = (bf16[1,512,4096]{2,1,0:T(8,128)(2,1)S(1)}, bf16[1,512,4096]{2,1,0:T(8,128)(2,1)}, u32[]{:S(2)}) copy-start(bf16[1,512,4096]{2,1,0:T(8,128)(2,1)} %param.15) | copy-start | bytes 12582916
  370.7 10.3 %copy-start.11 = (bf16[1,512,4096]{2,1,0:T(8,128)(2,1)S(1)}, bf16[1,512,4096]{2,1,0:T(8,128)(2,1)}, u32[]{:S(2)}) copy-start(bf16[1,512,4096]{2,1,0:T(8,128)(2,1)} %param.17) | copy-start | bytes 12582916
  432.6 12.5 %all-to-all-start = ((bf16[16,32,256]{2,1,0:T(8,128)(2,1)}), bf16[16,32,256]{2,1,0:T(8,128)(2,1)S(1)}, u32[]{:S(2)}, u32[]{:S(2)}) async-start(bf16[16,32,256]{2,1,0:T(8,128)(2,1)} %bitcast.431), calls=%async_computation.1 | async-start | bytes 524288 | tf_op jit(solution)/shard_map/all_to_all | solution.py:46
Sparse Core Ops, SparseCore 0:
  9.7 36.3 all-gather.6
  53.7 107.3 all-gather.8
  163.5 105.0 all-gather.10
  361.2 71.4 reduce-scatter.1
where the time goes:
time: 460 us; the launch traced here: 453 us
  waiting for transfers between devices  145 us (32%)
  local copies, waits for them, and re-layouts  99.8 us (22%)
  matrix products  97.3 us (21%)
  other arithmetic  66.7 us (14%)
  blocking collectives  23.2 us (5%)
  between operations  14.3 us (3%)
    all_gather x2, waiting for transfers between devices, carried_in(): lax.all_gather(a.astype(kind), axis)  71.9 us
    reduce_scatter x1, waiting for transfers between devices, shards(): lax.psum_scatter(lax.dot_general(features, projected_low, (((0,), (0,)),...  47.2 us
    dot_general x6, matrix products, group_pass(): within = jnp.einsum('hts,shp->thp', mix_weights, inputs)  40.4 us
    dynamic_update_slice x12, local copies, waits for them, and re-layouts, run_rows(): lax.scan(step_block, start_state, (features, entry_key, readout, log_bloc...  30.1 us
    all_gather x1, waiting for transfers between devices, shards(): weights_full = lax.all_gather(state_weights, 'fsdp', axis=0, tiled=True)  24.9 us
    all_gather x1, blocking collectives, carried_in(): lax.all_gather(a.astype(kind), axis)  23.2 us
    dot_general x6, matrix products, group_pass(): jnp.einsum('tn,hpn->thp', readout, state_now) * jnp.exp(running)[:, :, None]  22.2 us
    dynamic_update_slice x6, other arithmetic, run_rows(): lax.scan(step_block, start_state, (features, entry_key, readout, log_bloc...  20.5 us
  transfers between devices with their start and end apart: 5, of which 4 were waited for; matrix products, arithmetic and copies ran while one was open for 34% of the time, Pallas kernels for 0%

commit v1 on v0

v1 whole, which is shorter than its diff:
```python
import jax
import jax.numpy as jnp
from jax import lax
from jax.experimental import pallas as pl
from jax.experimental.pallas import tpu as pltpu
from jax.sharding import PartitionSpec as P

MESH = pl.DeviceIdType.MESH
F32 = jnp.float32
BF = jnp.bfloat16
T = 512
D = 4096
H = 32
N = 128
Q = 512
EPS = 1e-05
UNIT = 1.0 / 4096.0
RN = N ** (-0.5)
SEQ = 8
FS = 16


def dot(a, b):
    return jnp.dot(a, b, preferred_element_type=F32)


def dot_nt(a, b):
    return lax.dot_general(a, b, (((1,), (1,)), ((), ())), preferred_element_type=F32)


def dot_tn(a, b):
    return lax.dot_general(a, b, (((0,), (0,)), ((), ())), preferred_element_type=F32)


def split(v, parts):
    out = []
    for _ in range(parts):
        p = v.astype(BF)
        out.append(p)
        v = v - p.astype(F32)
    return jnp.concatenate(out, axis=1)


def pick(parts, head, heads):
    rows = lax.broadcasted_iota(jnp.int32, (parts * H, heads * N), 0)
    cols = lax.broadcasted_iota(jnp.int32, (parts * H, heads * N), 1)
    return (rows % H == head + cols // N).astype(F32).astype(BF)


def decays(ld):
    v = ld.astype(F32)
    hi = jnp.floor(v * (1.0 / 64.0))
    lo = v - hi * 64.0
    low = lax.broadcasted_iota(jnp.int32, (T, T), 0) >= lax.broadcasted_iota(
        jnp.int32, (T, T), 1
    )
    low = low.astype(F32).astype(BF)
    run = (64.0 * dot(low, hi.astype(BF)) + dot(low, lo.astype(BF))) * UNIT
    feed = jnp.sqrt(1.0 - jnp.exp(2.0 * (v * UNIT)))
    return run, feed


def kernel_a(
    x_ref, g_ref, ld_ref, w_ref,
    X_o, W_o, proj_o, AT_o, GT_o, dec_o, runs_o, lead_o, tail_o, feed_o, runT_o,
    wbuf, ss, rs, cs, cr,
):
    s = lax.axis_index("seq")
    f = lax.axis_index("fsdp")
    sib = f + 1 - 2 * (f % 2)
    barrier = pltpu.get_barrier_semaphore()
    for k in range(1, 8):
        pl.semaphore_signal(
            barrier, inc=1, device_id=(s, (f + 2 * k) % FS), device_id_type=MESH
        )
    pl.semaphore_signal(barrier, inc=1, device_id=(s, sib), device_id_type=MESH)
    pl.semaphore_wait(barrier, 8)

    def slot(i):
        return wbuf.at[pl.ds(pl.multiple_of(i * 256, 256), 256)]

    sends = []
    for k in range(1, 8):
        c = pltpu.make_async_remote_copy(
            w_ref, slot(f), ss.at[k - 1], rs.at[k - 1],
            device_id=(s, (f + 2 * k) % FS), device_id_type=MESH,
        )
        c.start()
        sends.append(c)
    own = pltpu.make_async_remote_copy(
        w_ref, slot(f), cs.at[0], cr.at[0], device_id=(s, sib), device_id_type=MESH
    )
    own.start()
    wbuf[pl.ds(pl.multiple_of(f * 256, 256), 256), :] = w_ref[...]

    def norm(i, _):
        rows = pl.ds(pl.multiple_of(i * 32, 32), 32)
        v = x_ref[rows, :].astype(F32)
        r = lax.rsqrt(jnp.mean(v * v, axis=1, keepdims=True) + EPS)
        X_o[rows, :] = (v * r).astype(BF)
        return 0

    lax.fori_loop(0, T // 32, norm, 0)

    run, feed = decays(ld_ref[...])
    end = run[T - 1 : T, :]
    runs_o[...] = split(run, 3)
    lead_o[...] = split(jnp.exp(run), 2)
    tail_o[...] = split(feed * jnp.exp(end - run), 2)
    feed_o[...] = split(feed, 2)
    wide = jnp.concatenate([run, jnp.zeros((T, N - H), F32)], axis=1)
    runT_o[...] = wide.T[:H, :]
    total = split(jnp.broadcast_to(jnp.exp(end), (8, H)), 3)
    for i in range(8):
        dec_o[:, i * Q : (i + 1) * Q] = dot(total, pick(3, 4 * i, 4))

    passed = []
    for k in range(1, 8):
        sends[k - 1].wait_recv()
        at = (f + FS - 2 * k) % FS
        c = pltpu.make_async_remote_copy(
            slot(at), slot(at), cs.at[k], cr.at[k],
            device_id=(s, sib), device_id_type=MESH,
        )
        c.start()
        passed.append(c)
    own.wait()
    for c in passed:
        c.wait()
    for c in sends:
        c.wait_send()

    def project(i, _):
        rows = pl.ds(pl.multiple_of(i * 128, 128), 128)
        proj_o[rows, :] = dot(X_o[rows, :], wbuf[...]).astype(BF)
        return 0

    lax.fori_loop(0, 4, project, 0)
    W_o[...] = wbuf[...]
    BT = proj_o[:, :N].astype(F32).T.astype(BF)
    CT = proj_o[:, N:].astype(F32).T.astype(BF)

    def states(i, _):
        cols = pl.ds(pl.multiple_of(i * Q, Q), Q)
        sel = pick(2, 4 * i, 4)
        xs = (X_o[:, cols].astype(F32) * dot(tail_o[...], sel)).astype(BF)
        AT_o[:, cols] = dot(BT, xs).astype(BF)
        gs = (g_ref[:, cols].astype(F32) * dot(lead_o[...], sel)).astype(BF)
        GT_o[:, cols] = (dot(CT, gs) * RN).astype(BF)
        return 0

    lax.fori_loop(0, 8, states, 0)


def kernel_b(
    gain_ref, X_ref, g_ref, proj_ref, AT_ref, GT_ref, dec_ref, runs_ref, feed_ref, runT_ref,
    S_o, G_o, mix_o, dx_o, dS_o,
    sc, a_in, g_in, d_in, a_out, g_out, S_buf, G_buf,
    s1, r1, s2, r2, s3, r3, s4, r4, s5, r5,
):
    s = lax.axis_index("seq")
    f = lax.axis_index("fsdp")
    barrier = pltpu.get_barrier_semaphore()
    for k in range(1, SEQ):
        pl.semaphore_signal(
            barrier, inc=1, device_id=((s + k) % SEQ, f), device_id_type=MESH
        )
    pl.semaphore_wait(barrier, SEQ - 1)

    def part(ref, i):
        return ref.at[:, pl.ds(pl.multiple_of(i * Q, Q), Q)]

    def send(src, dst, a, b, k):
        c = pltpu.make_async_remote_copy(
            src, dst, a.at[k - 1], b.at[k - 1],
            device_id=((s + k) % SEQ, f), device_id_type=MESH,
        )
        c.start()
        return c

    mine = pl.ds(pl.multiple_of(s * Q, Q), Q)
    decs, first, second = [], [], []
    for k in range(1, SEQ):
        to = (s + k) % SEQ
        decs.append(send(part(dec_ref, to), d_in.at[s], s5, r5, k))
        first.append(send(part(AT_ref, to), a_in.at[s], s1, r1, k))
    for k in range(1, SEQ):
        to = (s + k) % SEQ
        second.append(send(part(GT_ref, to), g_in.at[s], s2, r2, k))
    a_in[pl.ds(s, 1)] = AT_ref[:, mine][None]
    g_in[pl.ds(s, 1)] = GT_ref[:, mine][None]
    d_in[pl.ds(s, 1)] = dec_ref[:, mine][None]

    B = proj_ref[:, :N]
    C = proj_ref[:, N:]
    sc[...] = dot_nt(C, B) * RN
    dS_o[...] = jnp.zeros_like(dS_o)
    tri = lax.broadcasted_iota(jnp.int32, (N, N), 0) >= lax.broadcasted_iota(
        jnp.int32, (N, N), 1
    )

    def head(h, _):
        cols = pl.ds(pl.multiple_of(h * N, N), N)
        gain = gain_ref[h]
        run_b = dot(runs_ref[...], pick(3, h, 1))
        feed_b = dot(feed_ref[...], pick(2, h, 1))
        x = X_ref[:, cols].astype(F32)
        xf = (x * feed_b).astype(BF)
        g = g_ref[:, cols]
        row = runT_ref[pl.ds(h, 1), :]
        w = [[None] * 4 for _ in range(4)]
        for i in range(4):
            ri = slice(i * N, (i + 1) * N)
            dP = dot_nt(g[ri], xf[: (i + 1) * N])
            for j in range(i + 1):
                rj = slice(j * N, (j + 1) * N)
                d = run_b[ri] - row[:, rj]
                if i == j:
                    e = jnp.where(tri, jnp.exp(jnp.minimum(d, 0.0)), 0.0)
                else:
                    e = jnp.exp(d)
                dS_o[ri, rj] += e * dP[:, rj]
                w[i][j] = (e * sc[ri, rj]).astype(BF)
            wi = w[i][0] if i == 0 else jnp.concatenate(w[i][: i + 1], axis=1)
            m = dot(wi, xf[: (i + 1) * N]) + gain * x[ri]
            mix_o[ri, cols] = m.astype(BF)
        for j in range(4):
            rj = slice(j * N, (j + 1) * N)
            wj = [w[i][j] for i in range(j, 4)]
            wj = wj[0] if len(wj) == 1 else jnp.concatenate(wj, axis=0)
            dx = dot_tn(wj, g[j * N :]) * feed_b[rj] + gain * g[rj].astype(F32)
            dx_o[rj, cols] = dx.astype(BF)
        return 0

    lax.fori_loop(0, H // 2, head, 0)

    for c in decs + first:
        c.wait()
    state = jnp.zeros((N, Q), F32)
    for j in range(SEQ):
        a_out[j] = state.astype(BF)
        if j < SEQ - 1:
            state = d_in[j, 0:1, :] * state + a_in[j].astype(F32)
    third = []
    for k in range(1, SEQ):
        to = (s + k) % SEQ
        third.append(send(a_out.at[to], part(S_buf, s), s3, r3, k))
    S_buf[:, mine] = a_out[pl.ds(s, 1)][0]

    lax.fori_loop(H // 2, H, head, 0)

    for c in second:
        c.wait()
    state = jnp.zeros((N, Q), F32)
    for j in range(SEQ - 1, -1, -1):
        g_out[j] = state.astype(BF)
        if j > 0:
            state = d_in[j, 0:1, :] * state + g_in[j].astype(F32)
    fourth = []
    for k in range(1, SEQ):
        to = (s + k) % SEQ
        fourth.append(send(g_out.at[to], part(G_buf, s), s4, r4, k))
    G_buf[:, mine] = g_out[pl.ds(s, 1)][0]
    for c in third:
        c.wait()
    S_o[...] = S_buf[...]
    for c in fourth:
        c.wait()
    G_o[...] = G_buf[...]


def kernel_c(
    X_ref, g_ref, mix_ref, dx_ref, new_ref, S_ref, G_ref, proj_ref, lead_ref, tail_ref, dS_ref,
    old_o, fg_o, pl_o, dB, dC,
):
    i = pl.program_id(0)

    @pl.when(i == 0)
    def _():
        dB[...] = jnp.zeros_like(dB)
        dC[...] = jnp.zeros_like(dC)

    B = proj_ref[:, :N]
    C = proj_ref[:, N:]
    sel = pick(2, 4 * i, 4)
    lead = dot(lead_ref[...], sel) * RN
    tail = dot(tail_ref[...], sel)
    S = S_ref[...]
    G = G_ref[...]
    mixed = dot(C, S) * lead + mix_ref[...].astype(F32)
    old_o[...] = (new_ref[...].astype(F32) - mixed).astype(BF)
    fg_o[...] = (dot(B, G) * tail + dx_ref[...].astype(F32)).astype(BF)
    gs = (g_ref[...].astype(F32) * lead).astype(BF)
    dC[...] += dot_nt(gs, S)
    xs = (X_ref[...].astype(F32) * tail).astype(BF)
    dB[...] += dot_nt(xs, G)

    @pl.when(i == pl.num_programs(0) - 1)
    def _():
        dS = (dS_ref[...] * RN).astype(BF)
        pl_o[:, N:] = (dC[...] + dot(dS, B)).astype(BF)
        pl_o[:, :N] = (dB[...] + dot_tn(dS, C)).astype(BF)


def kernel_d(
    X_ref, pl_ref, o_ref, part, r1buf, acc1, r2buf, acc2, r3buf, s1, r1, s2, r2, s3, r3
):
    s = lax.axis_index("seq")
    f = lax.axis_index("fsdp")
    core = f % 2
    chip = f // 2
    sib = f + 1 - 2 * core
    barrier = pltpu.get_barrier_semaphore()
    for k in range(1, 8):
        pl.semaphore_signal(
            barrier, inc=1, device_id=(s, (f + 2 * k) % FS), device_id_type=MESH
        )
        pl.semaphore_signal(
            barrier, inc=1, device_id=((s + k) % SEQ, f), device_id_type=MESH
        )
    pl.semaphore_signal(barrier, inc=1, device_id=(s, sib), device_id_type=MESH)
    pl.semaphore_wait(barrier, 15)

    low = pl_ref[...]

    def product(i, _):
        cols = pl.ds(pl.multiple_of(i * Q, Q), Q)
        v = dot_tn(X_ref[:, cols], low).astype(BF)
        part[pl.ds(i, 1)] = v.reshape(1, 8, 2, 32, 256)
        return 0

    lax.fori_loop(0, 8, product, 0)
    c = pltpu.make_async_remote_copy(
        part.at[:, :, 1 - core], r1buf, s1, r1,
        device_id=(s, sib), device_id_type=MESH,
    )
    c.start()
    c.wait()
    own = part[:, :, pl.ds(core, 1)].reshape(8, 8, 32, 256)
    acc1[...] = (own.astype(F32) + r1buf[...].astype(F32)).astype(BF)
    cs = []
    for k in range(1, 8):
        to = (chip + k) % 8
        c = pltpu.make_async_remote_copy(
            acc1.at[:, to], r2buf.at[k - 1], s2.at[k - 1], r2.at[k - 1],
            device_id=(s, (f + 2 * k) % FS), device_id_type=MESH,
        )
        c.start()
        cs.append(c)
    total = acc1[:, pl.ds(chip, 1)].reshape(8, 32, 256).astype(F32)
    for k in range(7):
        cs[k].wait()
        total += r2buf[k].astype(F32)
    acc2[...] = total.astype(BF)
    cs = []
    for k in range(1, 8):
        to = (s + k) % SEQ
        c = pltpu.make_async_remote_copy(
            acc2.at[to], r3buf.at[k - 1], s3.at[k - 1], r3.at[k - 1],
            device_id=(to, f), device_id_type=MESH,
        )
        c.start()
        cs.append(c)
    total = acc2[pl.ds(s, 1)].reshape(32, 256).astype(F32)
    for k in range(7):
        cs[k].wait()
        total += r3buf[k].astype(F32)
    o_ref[...] = total * (T * SEQ * FS) ** (-0.5)


def kernel_e(x_ref, fg_ref, pl_ref, cot_ref, W_ref, o_ref, ng):
    low = pl_ref[...]
    rows = low.shape[0]
    xx = jnp.zeros((rows, 1), F32)
    xg = jnp.zeros((rows, 1), F32)
    for i in range(8):
        cols = slice(i * Q, (i + 1) * Q)
        x = x_ref[:, cols].astype(F32)
        v = dot_nt(low, W_ref[cols, :]) + fg_ref[:, cols].astype(F32)
        ng[:, cols] = v
        xx += jnp.sum(x * x, axis=1, keepdims=True)
        xg += jnp.sum(x * v, axis=1, keepdims=True)
    r = lax.rsqrt(xx * (1.0 / D) + EPS)
    back = r * r * r * xg * (1.0 / D)
    for i in range(8):
        cols = slice(i * Q, (i + 1) * Q)
        x = x_ref[:, cols].astype(F32)
        o_ref[:, cols] = (
            cot_ref[:, cols].astype(F32) + (r * ng[:, cols] - back * x)
        ).astype(BF)


def shape(*dims, dtype=BF):
    return jax.ShapeDtypeStruct(dims, dtype)


VM = pl.BlockSpec(memory_space=pltpu.VMEM)
DMA = pltpu.SemaphoreType.DMA
LIMIT = 56 << 20


def shards(middle, newest, middle_cot, newest_cot, log_decay, weights, gain):
    x, new, cot, g, ld = middle[0], newest[0], middle_cot[0], newest_cot[0], log_decay[0]

    def remote(cid):
        return pltpu.CompilerParams(
            collective_id=cid, has_side_effects=True, vmem_limit_bytes=LIMIT
        )

    X, W, proj, AT, GT, dec, runs, lead, tail, feed, runT = pl.pallas_call(
        kernel_a,
        name="gather",
        out_shape=[
            shape(T, D), shape(D, 2 * N), shape(T, 2 * N), shape(N, D), shape(N, D),
            shape(8, D, dtype=F32), shape(T, 3 * H), shape(T, 2 * H), shape(T, 2 * H), shape(T, 2 * H),
            shape(H, T, dtype=F32),
        ],
        in_specs=[VM] * 4,
        out_specs=[VM] * 11,
        scratch_shapes=[
            pltpu.VMEM((D, 2 * N), BF), DMA((7,)), DMA((7,)), DMA((8,)), DMA((8,)),
        ],
        compiler_params=remote(0),
    )(x, g, ld, weights)

    S, G, mix, dx, dS = pl.pallas_call(
        kernel_b,
        name="exchange",
        out_shape=[shape(N, D), shape(N, D), shape(T, D), shape(T, D), shape(T, T, dtype=F32)],
        in_specs=[pl.BlockSpec(memory_space=pltpu.SMEM)] + [VM] * 9,
        out_specs=[VM] * 5,
        scratch_shapes=[
            pltpu.VMEM((T, T), F32),
            pltpu.VMEM((SEQ, N, Q), BF), pltpu.VMEM((SEQ, N, Q), BF), pltpu.VMEM((SEQ, 8, Q), F32),
            pltpu.VMEM((SEQ, N, Q), BF), pltpu.VMEM((SEQ, N, Q), BF),
            pltpu.VMEM((N, D), BF), pltpu.VMEM((N, D), BF),
        ] + [DMA((7,))] * 10,
        compiler_params=remote(1),
    )(gain, X, g, proj, AT, GT, dec, runs, feed, runT)

    def cols(rows):
        return pl.BlockSpec((rows, Q), lambda i: (0, i))

    def whole(a):
        return pl.BlockSpec(a.shape, lambda i: (0, 0))

    old, fg, low = pl.pallas_call(
        kernel_c,
        name="carried",
        grid=(8,),
        out_shape=[shape(T, D), shape(T, D), shape(T, 2 * N)],
        in_specs=[cols(T)] * 5 + [cols(N)] * 2 + [whole(proj), whole(lead), whole(tail), whole(dS)],
        out_specs=[cols(T), cols(T), pl.BlockSpec((T, 2 * N), lambda i: (0, 0))],
        scratch_shapes=[pltpu.VMEM((T, N), F32), pltpu.VMEM((T, N), F32)],
        compiler_params=pltpu.CompilerParams(vmem_limit_bytes=LIMIT),
    )(X, g, mix, dx, new, S, G, proj, lead, tail, dS)

    grad = pl.pallas_call(
        kernel_d,
        name="reduce",
        out_shape=shape(32, 2 * N, dtype=F32),
        in_specs=[VM] * 2,
        out_specs=VM,
        scratch_shapes=[
            pltpu.VMEM((8, 8, 2, 32, 256), BF), pltpu.VMEM((8, 8, 32, 256), BF),
            pltpu.VMEM((8, 8, 32, 256), BF), pltpu.VMEM((7, 8, 32, 256), BF),
            pltpu.VMEM((8, 32, 256), BF), pltpu.VMEM((7, 32, 256), BF),
            DMA, DMA, DMA((7,)), DMA((7,)), DMA((7,)), DMA((7,)),
        ],
        compiler_params=remote(2),
    )(X, low)

    R = 128
    rows = pl.BlockSpec((R, D), lambda i: (i, 0))
    out = pl.pallas_call(
        kernel_e,
        name="normback",
        grid=(T // R,),
        out_shape=shape(T, D),
        in_specs=[rows, rows, pl.BlockSpec((R, 2 * N), lambda i: (i, 0)), rows, whole(W)],
        out_specs=rows,
        scratch_shapes=[pltpu.VMEM((R, D), F32)],
        compiler_params=pltpu.CompilerParams(vmem_limit_bytes=LIMIT),
    )(x, fg, low, cot, W)
    return old[None], out[None], grad


def solution(mesh):
    return jax.shard_map(
        shards,
        mesh=mesh,
        in_specs=(P("fsdp", "seq", None),) * 5 + (P("fsdp", None), P()),
        out_specs=(P("fsdp", "seq", None), P("fsdp", "seq", None), P(("seq", "fsdp"), None)),
        check_vma=False,
    )
```

time: 460 us -> 166 us (0.36)
  Pallas kernels: 0 us -> 160 us
  waiting for transfers between devices: 145 us -> 0 us
  local copies, waits for them, and re-layouts: 99.8 us -> 2.29 us
  matrix products: 97.3 us -> 0 us
  other arithmetic: 66.7 us -> 0 us
  blocking collectives: 23.2 us -> 0 us
  between operations: 14.3 us -> 0.67 us
    pallas_call x0 -> x5, Pallas kernels: none -> 160 us  [the longest x1 64.3 us: shards(): pl.pallas_call(kernel_b, name='exchange', out_shape=[shape(N, D), shape(N...]
    dot_general x29 -> x0, matrix products: 97.3 us -> none  [the longest x6 40.4 us: group_pass(): within = jnp.einsum('hts,shp->thp', mix_weights, inputs)]
    all_gather x3 -> x0, waiting for transfers between devices: 96.8 us -> none  [the longest x2 71.9 us: carried_in(): lax.all_gather(a.astype(kind), axis)]
    reduce_scatter x1 -> x0, waiting for transfers between devices: 47.2 us -> none  [shards(): lax.psum_scatter(lax.dot_general(features, projected_low, (((0,), (0,)),...]
    dynamic_update_slice x12 -> x0, local copies, waits for them, and re-layouts: 30.1 us -> none  [run_rows(): lax.scan(step_block, start_state, (features, entry_key, readout, log_bloc...]
    convert_element_type x3 -> x0, local copies, waits for them, and re-layouts: 24.2 us -> none  [the longest x2 17 us: shards(): normed, norm_back = jax.vjp(normalize, middle_state[0].astype(jnp.float32))]
    all_gather x1 -> x0, blocking collectives: 23.2 us -> none  [carried_in(): lax.all_gather(a.astype(kind), axis)]
    dynamic_update_slice x6 -> x0, other arithmetic: 20.5 us -> none  [run_rows(): lax.scan(step_block, start_state, (features, entry_key, readout, log_bloc...]
  transfers between devices with their start and end apart: 5 -> 0, of which waited for: 4 -> 0; matrix products, arithmetic and copies ran while one was open for 34% -> 0% of each run, Pallas kernels for 0% -> 0%
where the time goes in v1:
time: 166 us; the launch traced here: 163 us
  Pallas kernels  160 us (96%)
  local copies, waits for them, and re-layouts  2.29 us (1%)
    pallas_call x1, Pallas kernels, shards(): pl.pallas_call(kernel_b, name='exchange', out_shape=[shape(N, D), shape(N...  64.3 us
    pallas_call x1, Pallas kernels, shards(): pl.pallas_call(kernel_d, name='reduce', out_shape=shape(32, 2 * N, dtype=...  34.1 us
    pallas_call x1, Pallas kernels, shards(): pl.pallas_call(kernel_a, name='gather', out_shape=[shape(T, D), shape(D,...  32.9 us
    pallas_call x1, Pallas kernels, shards(): pl.pallas_call(kernel_c, name='carried', grid=(8,), out_shape=[shape(T, D...  17.1 us
    pallas_call x1, Pallas kernels, shards(): pl.pallas_call(kernel_e, name='normback', grid=(T // R,), out_shape=shape...  11.2 us

profile of v1, /device:TPU:0, one launch (start us, length us, event | category | flops | bytes accessed | tf_op | source)
XLA Modules:
  0.0 162.6 jit_solution(17740261800007553037)
XLA Ops:
  0.6 1.7 %copy.10 = s32[1,512,32]{2,1,0:T(8,128)} copy(s32[1,512,32]{1,2,0:T(8,128)} %param.11) | data formatting | bytes 131072 | tf_op args[4]
  2.3 32.9 %gather.1 = (bf16[512,4096]{1,0:T(8,128)(2,1)}, bf16[4096,256]{1,0:T(8,128)(2,1)}, bf16[512,256]{1,0:T(8,128)(2,1)}, bf16[128,4096]{1,0:T(8,128)(2,1)}, bf16[128...) custom-call(bf16[512,4096]{1,0:T(8,128)(2,1)} %bitcast.10, ...), custom_call_target="tpu_custom_call" | custom-call | tf_op jit(solution)/shard_map/gather/pallas_call | solution.py:410
  35.2 64.3 %exchange.1 = (bf16[128,4096]{1,0:T(8,128)(2,1)}, bf16[128,4096]{1,0:T(8,128)(2,1)}, bf16[512,4096]{1,0:T(8,128)(2,1)}, bf16[512,4096]{1,0:T(8,128)(2,1)}, f32[512,512]{1,0:T(8,128)}) custom-call(f32[32]{0:T(128)} %gain_ref.1, bf16[512,4096]{1,0:T(8,128)(2,1)} %get-tuple-element.22.X_ref, bf16[512,4096]{1,0:T(8,128)(2,1)} %bitcast.8, ...), custom_call_target="tpu_custom_call" | custom-call | tf_op jit(solution)/shard_map/exchange/pallas_call | solution.py:426
  99.5 17.1 %carried.1 = (bf16[512,4096]{1,0:T(8,128)(2,1)}, bf16[512,4096]{1,0:T(8,128)(2,1)}, bf16[512,256]{1,0:T(8,128)(2,1)}) custom-call(bf16[512,4096]{1,0:T(8,128)(2,1)} %get-tuple-element.22.X_ref, bf16[512,4096]{1,0:T(8,128)(2,1)} %bitcast.9, bf16[512,4096]{1,0:T(8,128)(2,1)} %get-tuple-element.30.mix_ref, bf16[512,4096]{1,0:T(8,128)(2,1)} %get-tuple-element.31.dx_ref, ...), custom_call_target="tpu_custom_call" | custom-call | tf_op jit(solution)/shard_map/carried/pallas_call | solution.py:447
  116.6 34.1 %reduce.1 = f32[32,256]{1,0:T(8,128)} custom-call(bf16[512,4096]{1,0:T(8,128)(2,1)} %get-tuple-element.22.X_ref, bf16[512,256]{1,0:T(8,128)(2,1)} %get-tuple-element.39.pl_ref), custom_call_target="tpu_custom_call" | custom-call | tf_op jit(solution)/shard_map/reduce/pallas_call | solution.py:458
  150.7 0.0 copy-start
  150.8 11.2 %normback.1 = bf16[512,4096]{1,0:T(8,128)(2,1)} custom-call(bf16[512,4096]{1,0:T(8,128)(2,1)} %bitcast.11, bf16[512,4096]{1,0:T(8,128)(2,1)} %get-tuple-element.38.fg_ref, bf16[512,256]{1,0:T(8,128)(2,1)} %get-tuple-element.39.pl_ref, bf16[512,4096]{1,0:T(8,128)(2,1)} %bitcast.13, bf16[4096,256]{1,0:T(8,128)(2,1)} %get-tuple-element.40.W_ref), custom_call_target="tpu_custom_call" | custom-call | tf_op jit(solution)/shard_map/normback/pallas_call | solution.py:475
  162.0 0.0 copy-done
  162.0 0.6 copy.12
Async XLA Ops:
  150.7 11.2 %copy-start = (f32[32,256]{1,0:T(8,128)S(1)}, f32[32,256]{1,0:T(8,128)}, u32[]{:S(2)}) copy-start(f32[32,256]{1,0:T(8,128)} %reduce.1) | copy-start | bytes 98308

commit v2 on v1

v2 whole, which is shorter than its diff:
```python
import jax
import jax.numpy as jnp
from jax import lax
from jax.experimental import pallas as pl
from jax.experimental.pallas import tpu as pltpu
from jax.sharding import PartitionSpec as P

MESH = pl.DeviceIdType.MESH
F32 = jnp.float32
BF = jnp.bfloat16
T = 512
D = 4096
H = 32
N = 128
Q = 512
EPS = 1e-05
UNIT = 1.0 / 4096.0
RN = N ** (-0.5)
SEQ = 8
FS = 16


def dot(a, b):
    return jnp.dot(a, b, preferred_element_type=F32)


def dot_nt(a, b):
    return lax.dot_general(a, b, (((1,), (1,)), ((), ())), preferred_element_type=F32)


def dot_tn(a, b):
    return lax.dot_general(a, b, (((0,), (0,)), ((), ())), preferred_element_type=F32)


def split(v, parts):
    out = []
    for _ in range(parts):
        p = v.astype(BF)
        out.append(p)
        v = v - p.astype(F32)
    return jnp.concatenate(out, axis=1)


def pick(parts, head, heads):
    rows = lax.broadcasted_iota(jnp.int32, (parts * H, heads * N), 0)
    cols = lax.broadcasted_iota(jnp.int32, (parts * H, heads * N), 1)
    return (rows % H == head + cols // N).astype(F32).astype(BF)


def decays(ld):
    v = ld.astype(F32)
    hi = jnp.floor(v * (1.0 / 64.0))
    lo = v - hi * 64.0
    low = lax.broadcasted_iota(jnp.int32, (T, T), 0) >= lax.broadcasted_iota(
        jnp.int32, (T, T), 1
    )
    low = low.astype(F32).astype(BF)
    run = (64.0 * dot(low, hi.astype(BF)) + dot(low, lo.astype(BF))) * UNIT
    feed = jnp.sqrt(1.0 - jnp.exp(2.0 * (v * UNIT)))
    return run, feed


def whole_step(
    gain_ref, x_hbm, new_hbm, cot_hbm, g_hbm, ld_ref, w_ref,
    old_hbm, grad_hbm, dw_ref,
    xb, X, gb, nb, cb, W, r_ref, proj, AT, GT, dec, runs, lead_s, tail_s, feed_s, runT,
    sc, dS, mix, dx, a_in, g_in, d_in, a_out, g_out, S_buf, G_buf, dB, dC, low, ng,
    part, r1buf, acc1, r2buf, acc2, r3buf,
    lsem, osem, gsem, ss, rs, cs, cr, s1, r1, s2, r2, s3, r3, s4, r4, s5, r5,
    u1, v1, u2, v2, u3, v3,
):
    s = lax.axis_index("seq")
    f = lax.axis_index("fsdp")
    core = f % 2
    chip = f // 2
    sib = f + 1 - 2 * core

    loads = []
    for k, (a, b) in enumerate(((x_hbm, xb), (g_hbm, gb), (new_hbm, nb), (cot_hbm, cb))):
        c = pltpu.make_async_copy(a, b, lsem.at[k])
        c.start()
        loads.append(c)

    barrier = pltpu.get_barrier_semaphore()
    for k in range(1, 8):
        pl.semaphore_signal(
            barrier, inc=1, device_id=(s, (f + 2 * k) % FS), device_id_type=MESH
        )
        pl.semaphore_signal(
            barrier, inc=1, device_id=((s + k) % SEQ, f), device_id_type=MESH
        )
    pl.semaphore_signal(barrier, inc=1, device_id=(s, sib), device_id_type=MESH)
    pl.semaphore_wait(barrier, 15)

    def slot(i):
        return W.at[pl.ds(pl.multiple_of(i * 256, 256), 256)]

    sends = []
    for k in range(1, 8):
        c = pltpu.make_async_remote_copy(
            w_ref, slot(f), ss.at[k - 1], rs.at[k - 1],
            device_id=(s, (f + 2 * k) % FS), device_id_type=MESH,
        )
        c.start()
        sends.append(c)
    own = pltpu.make_async_remote_copy(
        w_ref, slot(f), cs.at[0], cr.at[0], device_id=(s, sib), device_id_type=MESH
    )
    own.start()
    W[pl.ds(pl.multiple_of(f * 256, 256), 256), :] = w_ref[...]

    run, feed = decays(ld_ref[...])
    end = run[T - 1 : T, :]
    runs[...] = split(run, 3)
    lead_s[...] = split(jnp.exp(run), 2)
    tail_s[...] = split(feed * jnp.exp(end - run), 2)
    feed_s[...] = split(feed, 2)
    wide = jnp.concatenate([run, jnp.zeros((T, N - H), F32)], axis=1)
    runT[...] = wide.T[:H, :]
    total = split(jnp.broadcast_to(jnp.exp(end), (8, H)), 3)
    for i in range(8):
        dec[i] = dot(total, pick(3, 4 * i, 4))

    loads[0].wait()

    def norm(i, _):
        rows = pl.ds(pl.multiple_of(i * 32, 32), 32)
        v = xb[rows, :].astype(F32)
        r = lax.rsqrt(jnp.mean(v * v, axis=1, keepdims=True) + EPS)
        r_ref[rows, :] = r
        X[rows, :] = (v * r).astype(BF)
        return 0

    lax.fori_loop(0, T // 32, norm, 0)

    passed = []
    for k in range(1, 8):
        sends[k - 1].wait_recv()
        at = (f + FS - 2 * k) % FS
        c = pltpu.make_async_remote_copy(
            slot(at), slot(at), cs.at[k], cr.at[k],
            device_id=(s, sib), device_id_type=MESH,
        )
        c.start()
        passed.append(c)
    loads[1].wait()
    own.wait()
    for c in passed:
        c.wait()

    def project(i, _):
        rows = pl.ds(pl.multiple_of(i * 128, 128), 128)
        proj[rows, :] = dot(X[rows, :], W[...]).astype(BF)
        return 0

    lax.fori_loop(0, 4, project, 0)
    B = proj[:, :N]
    C = proj[:, N:]
    BT = B.astype(F32).T.astype(BF)
    CT = C.astype(F32).T.astype(BF)

    def peer(src, dst, a, b, k):
        return pltpu.make_async_remote_copy(
            src, dst, a.at[k], b.at[k],
            device_id=((s + k) % SEQ, f), device_id_type=MESH,
        )

    def to_dec(k):
        return peer(dec.at[(s + k) % SEQ], d_in.at[s], s5, r5, k)

    def to_a(k):
        return peer(AT.at[(s + k) % SEQ], a_in.at[s], s1, r1, k)

    def to_g(k):
        return peer(GT.at[(s + k) % SEQ], g_in.at[s], s2, r2, k)

    def back_a(k):
        return peer(a_out.at[(s + k) % SEQ], S_buf.at[s], s3, r3, k)

    def back_g(k):
        return peer(g_out.at[(s + k) % SEQ], G_buf.at[s], s4, r4, k)

    def make_a(k, _):
        i = (s + k) % SEQ
        cols = pl.ds(pl.multiple_of(i * Q, Q), Q)
        sel = pick(2, 4 * i, 4)
        xs = (X[:, cols].astype(F32) * dot(tail_s[...], sel)).astype(BF)
        AT[i] = dot(BT, xs).astype(BF)

        @pl.when(k < SEQ)
        def _():
            to_dec(k).start()
            to_a(k).start()

        return 0

    def make_g(k, _):
        i = (s + k) % SEQ
        cols = pl.ds(pl.multiple_of(i * Q, Q), Q)
        sel = pick(2, 4 * i, 4)
        gs = (gb[:, cols].astype(F32) * dot(lead_s[...], sel)).astype(BF)
        GT[i] = (dot(CT, gs) * RN).astype(BF)

        @pl.when(k < SEQ)
        def _():
            to_g(k).start()

        return 0

    lax.fori_loop(1, SEQ + 1, make_a, 0)
    lax.fori_loop(1, SEQ + 1, make_g, 0)
    a_in[pl.ds(s, 1)] = AT[pl.ds(s, 1)]
    g_in[pl.ds(s, 1)] = GT[pl.ds(s, 1)]
    d_in[pl.ds(s, 1)] = dec[pl.ds(s, 1)]

    sc[...] = dot_nt(C, B) * RN
    dS[...] = jnp.zeros_like(dS)
    dB[...] = jnp.zeros_like(dB)
    dC[...] = jnp.zeros_like(dC)
    tri = lax.broadcasted_iota(jnp.int32, (N, N), 0) >= lax.broadcasted_iota(
        jnp.int32, (N, N), 1
    )

    def head(h, _):
        cols = pl.ds(pl.multiple_of(h * N, N), N)
        gain = gain_ref[h]
        run_b = dot(runs[...], pick(3, h, 1))
        feed_b = dot(feed_s[...], pick(2, h, 1))
        x = X[:, cols].astype(F32)
        xf = (x * feed_b).astype(BF)
        g = gb[:, cols]
        row = runT[pl.ds(h, 1), :]
        w = [[None] * 4 for _ in range(4)]
        for i in range(4):
            ri = slice(i * N, (i + 1) * N)
            dP = dot_nt(g[ri], xf[: (i + 1) * N])
            for j in range(i + 1):
                rj = slice(j * N, (j + 1) * N)
                d = run_b[ri] - row[:, rj]
                if i == j:
                    e = jnp.where(tri, jnp.exp(jnp.minimum(d, 0.0)), 0.0)
                else:
                    e = jnp.exp(d)
                dS[ri, rj] += e * dP[:, rj]
                w[i][j] = (e * sc[ri, rj]).astype(BF)
            wi = w[i][0] if i == 0 else jnp.concatenate(w[i][: i + 1], axis=1)
            m = dot(wi, xf[: (i + 1) * N]) + gain * x[ri]
            mix[ri, cols] = m.astype(BF)
        for j in range(4):
            rj = slice(j * N, (j + 1) * N)
            wj = [w[i][j] for i in range(j, 4)]
            wj = wj[0] if len(wj) == 1 else jnp.concatenate(wj, axis=0)
            v = dot_tn(wj, g[j * N :]) * feed_b[rj] + gain * g[rj].astype(F32)
            dx[rj, cols] = v.astype(BF)
        return 0

    def wait_in(make):
        def one(k, _):
            make(k).wait()
            return 0

        lax.fori_loop(1, SEQ, one, 0)

    def start_back(make):
        def one(k, _):
            make(k).start()
            return 0

        lax.fori_loop(1, SEQ, one, 0)

    lax.fori_loop(0, HEADS_1, head, 0)

    wait_in(to_dec)
    wait_in(to_a)
    state = jnp.zeros((N, Q), F32)
    for j in range(SEQ):
        a_out[j] = state.astype(BF)
        if j < SEQ - 1:
            state = d_in[j, 0:1, :] * state + a_in[j].astype(F32)
    start_back(back_a)
    S_buf[pl.ds(s, 1)] = a_out[pl.ds(s, 1)]

    lax.fori_loop(HEADS_1, HEADS_2, head, 0)

    wait_in(to_g)
    state = jnp.zeros((N, Q), F32)
    for j in range(SEQ - 1, -1, -1):
        g_out[j] = state.astype(BF)
        if j > 0:
            state = d_in[j, 0:1, :] * state + g_in[j].astype(F32)
    start_back(back_g)
    G_buf[pl.ds(s, 1)] = g_out[pl.ds(s, 1)]

    lax.fori_loop(HEADS_2, H, head, 0)
    loads[2].wait()

    def old_copy(i):
        cols = pl.ds(pl.multiple_of(i * Q, Q), Q)
        return pltpu.make_async_copy(nb.at[:, cols], old_hbm.at[:, cols], osem.at[i])

    def carried(k, _):
        @pl.when(k > 0)
        def _():
            back_a(k).wait()

        i = (s + SEQ - k) % SEQ
        cols = pl.ds(pl.multiple_of(i * Q, Q), Q)
        lead = dot(lead_s[...], pick(2, 4 * i, 4)) * RN
        S = S_buf[i]
        mixed = dot(C, S) * lead + mix[:, cols].astype(F32)
        nb[:, cols] = (nb[:, cols].astype(F32) - mixed).astype(BF)
        old_copy(i).start()
        gs = (gb[:, cols].astype(F32) * lead).astype(BF)
        dC[...] += dot_nt(gs, S)
        return 0

    lax.fori_loop(0, SEQ, carried, 0)

    dSl = (dS[...] * RN).astype(BF)
    low[:, N:] = (dC[...] + dot(dSl, B)).astype(BF)
    dB[...] = dot_tn(dSl, C)

    def carried_back(k, _):
        @pl.when(k > 0)
        def _():
            back_g(k).wait()

        i = (s + SEQ - k) % SEQ
        cols = pl.ds(pl.multiple_of(i * Q, Q), Q)
        tail = dot(tail_s[...], pick(2, 4 * i, 4))
        G = G_buf[i]
        xs = (X[:, cols].astype(F32) * tail).astype(BF)
        dB[...] += dot_nt(xs, G)
        dx[:, cols] = (dot(B, G) * tail + dx[:, cols].astype(F32)).astype(BF)
        return 0

    lax.fori_loop(0, SEQ, carried_back, 0)
    low[:, :N] = dB[...].astype(BF)

    def to_sib(i):
        return pltpu.make_async_remote_copy(
            part.at[i, :, 1 - core], r1buf.at[i], u1.at[i], v1.at[i],
            device_id=(s, sib), device_id_type=MESH,
        )

    def product(i, _):
        cols = pl.ds(pl.multiple_of(i * Q, Q), Q)
        v = dot_tn(X[:, cols], low[...]).astype(BF)
        part[pl.ds(i, 1)] = v.reshape(1, 8, 2, 32, 256)
        to_sib(i).start()
        return 0

    lax.fori_loop(0, SEQ, product, 0)

    def join(i, _):
        to_sib(i).wait()
        mine = part[pl.ds(i, 1), :, pl.ds(core, 1)].reshape(8, 32, 256)
        acc1[i] = (mine.astype(F32) + r1buf[i].astype(F32)).astype(BF)
        return 0

    lax.fori_loop(0, SEQ, join, 0)

    def to_chip(k):
        return pltpu.make_async_remote_copy(
            acc1.at[:, (chip + k) % 8], r2buf.at[k - 1], u2.at[k - 1], v2.at[k - 1],
            device_id=(s, (f + 2 * k) % FS), device_id_type=MESH,
        )

    for k in range(1, 8):
        to_chip(k).start()

    loads[3].wait()

    def grad_copy(b):
        rows = pl.ds(pl.multiple_of(b * 128, 128), 128)
        return pltpu.make_async_copy(cb.at[rows], grad_hbm.at[rows], gsem.at[b])

    def normback(b, _):
        rows = pl.ds(pl.multiple_of(b * 128, 128), 128)
        lo = low[rows, :]
        xg = jnp.zeros((128, N), F32)
        for i in range(8):
            cols = slice(i * Q, (i + 1) * Q)
            v = dot_nt(lo, W[cols, :]) + dx[rows, cols].astype(F32)
            ng[:, cols] = v
            t = xb[rows, cols].astype(F32) * v
            xg += t[:, :N] + t[:, N : 2 * N] + t[:, 2 * N : 3 * N] + t[:, 3 * N :]
        r = r_ref[rows, :]
        back = r * r * r * (jnp.sum(xg, axis=1, keepdims=True) * (1.0 / D))
        for i in range(8):
            cols = slice(i * Q, (i + 1) * Q)
            v = r * ng[:, cols] - back * xb[rows, cols].astype(F32)
            cb[rows, cols] = (cb[rows, cols].astype(F32) + v).astype(BF)
        grad_copy(b).start()
        return 0

    lax.fori_loop(0, 4, normback, 0)

    total = acc1[:, pl.ds(chip, 1)].reshape(8, 32, 256).astype(F32)
    for k in range(1, 8):
        to_chip(k).wait()
        total += r2buf[k - 1].astype(F32)
    acc2[...] = total.astype(BF)

    def to_seq(k):
        return pltpu.make_async_remote_copy(
            acc2.at[(s + k) % SEQ], r3buf.at[k - 1], u3.at[k - 1], v3.at[k - 1],
            device_id=((s + k) % SEQ, f), device_id_type=MESH,
        )

    for k in range(1, 8):
        to_seq(k).start()
    for c in sends:
        c.wait_send()
    for i in range(SEQ):
        old_copy(i).wait()
    for b in range(4):
        grad_copy(b).wait()
    total = acc2[pl.ds(s, 1)].reshape(32, 256).astype(F32)
    for k in range(1, 8):
        to_seq(k).wait()
        total += r3buf[k - 1].astype(F32)
    dw_ref[...] = total * (T * SEQ * FS) ** (-0.5)


def shape(*dims, dtype=BF):
    return jax.ShapeDtypeStruct(dims, dtype)


HEADS_1 = 12
HEADS_2 = 24
VM = pl.BlockSpec(memory_space=pltpu.VMEM)
ANY = pl.BlockSpec(memory_space=pl.ANY)
DMA = pltpu.SemaphoreType.DMA
LIMIT = 60 << 20


def shards(middle, newest, middle_cot, newest_cot, log_decay, weights, gain):
    def vm(*dims, dtype=BF):
        return pltpu.VMEM(dims, dtype)

    scratch = [
        vm(T, D), vm(T, D), vm(T, D), vm(T, D), vm(T, D), vm(D, 2 * N), vm(T, 1, dtype=F32),
        vm(T, 2 * N), vm(SEQ, N, Q), vm(SEQ, N, Q), vm(SEQ, 8, Q, dtype=F32),
        vm(T, 3 * H), vm(T, 2 * H), vm(T, 2 * H), vm(T, 2 * H), vm(H, T, dtype=F32),
        vm(T, T, dtype=F32), vm(T, T, dtype=F32), vm(T, D), vm(T, D),
        vm(SEQ, N, Q), vm(SEQ, N, Q), vm(SEQ, 8, Q, dtype=F32),
        vm(SEQ, N, Q), vm(SEQ, N, Q), vm(SEQ, N, Q), vm(SEQ, N, Q),
        vm(T, N, dtype=F32), vm(T, N, dtype=F32), vm(T, 2 * N), vm(128, D, dtype=F32),
        vm(8, 8, 2, 32, 256), vm(8, 8, 32, 256), vm(8, 8, 32, 256), vm(7, 8, 32, 256),
        vm(8, 32, 256), vm(7, 32, 256),
        DMA((4,)), DMA((8,)), DMA((4,)), DMA((7,)), DMA((7,)), DMA((8,)), DMA((8,)),
    ] + [DMA((8,))] * 10 + [DMA((8,)), DMA((8,))] + [DMA((7,))] * 4
    old, out, grad = pl.pallas_call(
        whole_step,
        name="step",
        out_shape=[shape(T, D), shape(T, D), shape(32, 2 * N, dtype=F32)],
        in_specs=[pl.BlockSpec(memory_space=pltpu.SMEM)] + [ANY] * 4 + [VM] * 2,
        out_specs=[ANY, ANY, VM],
        scratch_shapes=scratch,
        compiler_params=pltpu.CompilerParams(
            collective_id=0, has_side_effects=True, vmem_limit_bytes=LIMIT
        ),
    )(gain, middle[0], newest[0], middle_cot[0], newest_cot[0], log_decay[0], weights)
    return old[None], out[None], grad


def solution(mesh):
    return jax.shard_map(
        shards,
        mesh=mesh,
        in_specs=(P("fsdp", "seq", None),) * 5 + (P("fsdp", None), P()),
        out_specs=(P("fsdp", "seq", None), P("fsdp", "seq", None), P(("seq", "fsdp"), None)),
        check_vma=False,
    )
```

time: 166 us -> 116 us (0.70); the launches traced: 163 us -> 115 us
  Pallas kernels: 160 us -> 105 us
  local copies, waits for them, and re-layouts: 2.29 us -> 9.16 us
    pallas_call x5 -> x1, Pallas kernels: 160 us -> 105 us  [shards(): pl.pallas_call(whole_step, name='step', out_shape=[shape(T, D), shape(T,...]
    unnamed x4 -> x8, local copies, waits for them, and re-layouts: 2.29 us -> 9.16 us
where the time goes in v2:
time: 116 us; the launch traced here: 115 us
  Pallas kernels  105 us (91%)
  local copies, waits for them, and re-layouts  9.16 us (8%)
    pallas_call x1, Pallas kernels, shards(): pl.pallas_call(whole_step, name='step', out_shape=[shape(T, D), shape(T,...  105 us
    unnamed x8, local copies, waits for them, and re-layouts  9.16 us

profile of v2, /device:TPU:0, one launch (start us, length us, event | category | flops | bytes accessed | tf_op | source)
XLA Modules:
  0.0 115.0 jit_solution(12366093542181111224)
XLA Ops:
  0.6 1.7 %copy.10 = s32[1,512,32]{2,1,0:T(8,128)} copy(s32[1,512,32]{1,2,0:T(8,128)} %param.11) | data formatting | bytes 131072 | tf_op args[4]
  2.3 105.2 %step.1 = (bf16[512,4096]{1,0:T(8,128)(2,1)}, bf16[512,4096]{1,0:T(8,128)(2,1)}, f32[32,256]{1,0:T(8,128)}) custom-call(f32[32]{0:T(128)} %gain_ref.1, bf16[512,4096]{1,0:T(8,128)(2,1)} %bitcast.7, bf16[512,4096]{1,0:T(8,128)(2,1)} %bitcast.8, bf16[512,4096]{1,0:T(8,128)(2,1)} %bitcast.9, bf16[512,4096]{1,0:T(8,128)(2,1)} %bitcast.10, s32[512,32]{1,0:T(8,128)} %bitcast.13, ...), custom_call_target="tpu_custom_call" | custom-call | tf_op jit(solution)/shard_map/step/pallas_call | solution.py:454
  107.5 0.0 copy-start
  107.5 4.8 %copy.14 = bf16[1,512,4096]{2,1,0:T(8,128)(2,1)} copy(bf16[1,512,4096]{2,1,0:T(8,128)(2,1)} %bitcast.12) | data formatting | bytes 8388608
  112.3 0.0 copy-done
  112.3 0.0 copy-start.1
  112.3 2.0 %copy.15 = bf16[1,512,4096]{2,1,0:T(8,128)(2,1)} copy(bf16[1,512,4096]{2,1,0:T(8,128)(2,1)S(1)} %bitcast.11) | data formatting | bytes 8388608
  114.4 0.0 copy-done.1
  114.4 0.6 copy.16
Async XLA Ops:
  107.5 4.9 %copy-start = (bf16[512,4096]{1,0:T(8,128)(2,1)S(1)}, bf16[512,4096]{1,0:T(8,128)(2,1)}, u32[]{:S(2)}) copy-start(bf16[512,4096]{1,0:T(8,128)(2,1)} %get-tuple-element.7) | copy-start | bytes 12582916
  112.3 2.0 %copy-start.1 = (f32[32,256]{1,0:T(8,128)S(1)}, f32[32,256]{1,0:T(8,128)}, u32[]{:S(2)}) copy-start(f32[32,256]{1,0:T(8,128)} %get-tuple-element.14) | copy-start | bytes 98308

commit v3 on v2

--- a/solution.py
+++ b/solution.py
@@ -51,22 +51,22 @@
     v = ld.astype(F32)
     hi = jnp.floor(v * (1.0 / 64.0))
     lo = v - hi * 64.0
-    low = lax.broadcasted_iota(jnp.int32, (T, T), 0) >= lax.broadcasted_iota(
+    up = lax.broadcasted_iota(jnp.int32, (T, T), 0) <= lax.broadcasted_iota(
         jnp.int32, (T, T), 1
     )
-    low = low.astype(F32).astype(BF)
-    run = (64.0 * dot(low, hi.astype(BF)) + dot(low, lo.astype(BF))) * UNIT
+    up = up.astype(F32).astype(BF)
+    run = (64.0 * dot(hi.astype(BF), up) + dot(lo.astype(BF), up)) * UNIT
     feed = jnp.sqrt(1.0 - jnp.exp(2.0 * (v * UNIT)))
     return run, feed
 
 
 def whole_step(
     gain_ref, x_hbm, new_hbm, cot_hbm, g_hbm, ld_ref, w_ref,
-    old_hbm, grad_hbm, dw_ref,
-    xb, X, gb, nb, cb, W, r_ref, proj, AT, GT, dec, runs, lead_s, tail_s, feed_s, runT,
-    sc, dS, mix, dx, a_in, g_in, d_in, a_out, g_out, S_buf, G_buf, dB, dC, low, ng,
+    nb, cb, dw_ref,
+    xb, X, XT, gb, W, r_ref, proj, AT, GT, dec, runs, lead_s, tail_s, feed_s, runT, leadT, tailT,
+    sc, dS, mix, dx, a_in, g_in, d_in, a_out, g_out, S_buf, G_buf, dB, dC, low, ng, side,
     part, r1buf, acc1, r2buf, acc2, r3buf,
-    lsem, osem, gsem, ss, rs, cs, cr, s1, r1, s2, r2, s3, r3, s4, r4, s5, r5,
+    lsem, ss, rs, cs, cr, s1, r1, s2, r2, s3, r3, s4, r4, s5, r5,
     u1, v1, u2, v2, u3, v3,
 ):
     s = lax.axis_index("seq")
@@ -95,28 +95,40 @@
     def slot(i):
         return W.at[pl.ds(pl.multiple_of(i * 256, 256), 256)]
 
-    sends = []
-    for k in range(1, 8):
-        c = pltpu.make_async_remote_copy(
-            w_ref, slot(f), ss.at[k - 1], rs.at[k - 1],
+    def half(ref, p):
+        return ref.at[:, pl.ds(p * N, N)]
+
+    def to_peer(p, k):
+        return pltpu.make_async_remote_copy(
+            half(w_ref, p), half(slot(f), p), ss.at[p, k], rs.at[p, k],
             device_id=(s, (f + 2 * k) % FS), device_id_type=MESH,
         )
-        c.start()
-        sends.append(c)
-    own = pltpu.make_async_remote_copy(
-        w_ref, slot(f), cs.at[0], cr.at[0], device_id=(s, sib), device_id_type=MESH
-    )
-    own.start()
+
+    def on(p, k):
+        at = slot((f + FS - 2 * k) % FS)
+        return pltpu.make_async_remote_copy(
+            half(w_ref if k == 0 else at, p), half(at, p), cs.at[p, k], cr.at[p, k],
+            device_id=(s, sib), device_id_type=MESH,
+        )
+
+    for p in range(2):
+        for k in range(1, 8):
+            to_peer(p, k).start()
+        on(p, 0).start()
     W[pl.ds(pl.multiple_of(f * 256, 256), 256), :] = w_ref[...]
 
-    run, feed = decays(ld_ref[...])
+    run_rows, feed_rows = decays(ld_ref[...])
+    runT[...] = run_rows
+    leadT[...] = jnp.exp(run_rows)
+    tailT[...] = feed_rows * jnp.exp(run_rows[:, T - 1 :] - run_rows)
+    fill = jnp.zeros((N - H, T), F32)
+    run = jnp.concatenate([run_rows, fill], axis=0).T[:, :H]
+    feed = jnp.concatenate([feed_rows, fill], axis=0).T[:, :H]
     end = run[T - 1 : T, :]
     runs[...] = split(run, 3)
     lead_s[...] = split(jnp.exp(run), 2)
     tail_s[...] = split(feed * jnp.exp(end - run), 2)
     feed_s[...] = split(feed, 2)
-    wide = jnp.concatenate([run, jnp.zeros((T, N - H), F32)], axis=1)
-    runT[...] = wide.T[:H, :]
     total = split(jnp.broadcast_to(jnp.exp(end), (8, H)), 3)
     for i in range(8):
         dec[i] = dot(total, pick(3, 4 * i, 4))
@@ -133,31 +145,19 @@
 
     lax.fori_loop(0, T // 32, norm, 0)
 
-    passed = []
-    for k in range(1, 8):
-        sends[k - 1].wait_recv()
-        at = (f + FS - 2 * k) % FS
-        c = pltpu.make_async_remote_copy(
-            slot(at), slot(at), cs.at[k], cr.at[k],
-            device_id=(s, sib), device_id_type=MESH,
-        )
-        c.start()
-        passed.append(c)
-    loads[1].wait()
-    own.wait()
-    for c in passed:
-        c.wait()
-
-    def project(i, _):
-        rows = pl.ds(pl.multiple_of(i * 128, 128), 128)
-        proj[rows, :] = dot(X[rows, :], W[...]).astype(BF)
-        return 0
-
-    lax.fori_loop(0, 4, project, 0)
-    B = proj[:, :N]
-    C = proj[:, N:]
-    BT = B.astype(F32).T.astype(BF)
-    CT = C.astype(F32).T.astype(BF)
+    def gathered(p):
+        for k in range(1, 8):
+            to_peer(p, k).wait_recv()
+            on(p, k).start()
+        for k in range(8):
+            on(p, k).wait()
+
+    def project(p):
+        cols = slice(p * N, (p + 1) * N)
+        for i in range(4):
+            rows = slice(i * 128, (i + 1) * 128)
+            proj[rows, cols] = dot(X[rows, :], W[:, cols]).astype(BF)
+        return proj[:, cols].astype(F32).T
 
     def peer(src, dst, a, b, k):
         return pltpu.make_async_remote_copy(
@@ -180,12 +180,16 @@
     def back_g(k):
         return peer(g_out.at[(s + k) % SEQ], G_buf.at[s], s4, r4, k)
 
+    gathered(0)
+    side[...] = project(0)
+
     def make_a(k, _):
         i = (s + k) % SEQ
-        cols = pl.ds(pl.multiple_of(i * Q, Q), Q)
-        sel = pick(2, 4 * i, 4)
-        xs = (X[:, cols].astype(F32) * dot(tail_s[...], sel)).astype(BF)
-        AT[i] = dot(BT, xs).astype(BF)
+        for q in range(4):
+            h = 4 * i + q
+            bs = (side[...] * tailT[pl.ds(h, 1), :]).astype(BF)
+            x = X[:, pl.ds(pl.multiple_of(h * N, N), N)]
+            AT[i, :, q * N : (q + 1) * N] = dot(bs, x).astype(BF)
 
         @pl.when(k < SEQ)
         def _():
@@ -194,12 +198,18 @@
 
         return 0
 
+    lax.fori_loop(1, SEQ + 1, make_a, 0)
+    gathered(1)
+    loads[1].wait()
+    side[...] = project(1) * RN
+
     def make_g(k, _):
         i = (s + k) % SEQ
-        cols = pl.ds(pl.multiple_of(i * Q, Q), Q)
-        sel = pick(2, 4 * i, 4)
-        gs = (gb[:, cols].astype(F32) * dot(lead_s[...], sel)).astype(BF)
-        GT[i] = (dot(CT, gs) * RN).astype(BF)
+        for q in range(4):
+            h = 4 * i + q
+            c = (side[...] * leadT[pl.ds(h, 1), :]).astype(BF)
+            g = gb[:, pl.ds(pl.multiple_of(h * N, N), N)]
+            GT[i, :, q * N : (q + 1) * N] = dot(c, g).astype(BF)
 
         @pl.when(k < SEQ)
         def _():
@@ -207,8 +217,9 @@
 
         return 0
 
-    lax.fori_loop(1, SEQ + 1, make_a, 0)
     lax.fori_loop(1, SEQ + 1, make_g, 0)
+    B = proj[:, :N]
+    C = proj[:, N:]
     a_in[pl.ds(s, 1)] = AT[pl.ds(s, 1)]
     g_in[pl.ds(s, 1)] = GT[pl.ds(s, 1)]
     d_in[pl.ds(s, 1)] = dec[pl.ds(s, 1)]
@@ -227,6 +238,7 @@
         run_b = dot(runs[...], pick(3, h, 1))
         feed_b = dot(feed_s[...], pick(2, h, 1))
         x = X[:, cols].astype(F32)
+        XT[cols, :] = x.T.astype(BF)
         xf = (x * feed_b).astype(BF)
         g = gb[:, cols]
         row = runT[pl.ds(h, 1), :]
@@ -294,9 +306,40 @@
     lax.fori_loop(HEADS_2, H, head, 0)
     loads[2].wait()
 
-    def old_copy(i):
-        cols = pl.ds(pl.multiple_of(i * Q, Q), Q)
-        return pltpu.make_async_copy(nb.at[:, cols], old_hbm.at[:, cols], osem.at[i])
+    def to_sib(p, i):
+        return pltpu.make_async_remote_copy(
+            part.at[p, i, :, 1 - core], r1buf.at[p, i], u1.at[p, i], v1.at[p, i],
+            device_id=(s, sib), device_id_type=MESH,
+        )
+
+    def to_chip(p, k):
+        return pltpu.make_async_remote_copy(
+            acc1.at[p, :, (chip + k) % 8], r2buf.at[p, k - 1], u2.at[p, k - 1], v2.at[p, k - 1],
+            device_id=(s, (f + 2 * k) % FS), device_id_type=MESH,
+        )
+
+    def product(p):
+        half_low = low[:, p * N : (p + 1) * N]
+
+        def one(i, _):
+            rows = pl.ds(pl.multiple_of(i * Q, Q), Q)
+            v = dot(XT[rows, :], half_low).astype(BF)
+            part[p, pl.ds(i, 1)] = v.reshape(1, 8, 2, 32, N)
+            to_sib(p, i).start()
+            return 0
+
+        lax.fori_loop(0, SEQ, one, 0)
+
+    def join(p):
+        def one(i, _):
+            to_sib(p, i).wait()
+            mine = part[p, pl.ds(i, 1), :, pl.ds(core, 1)].reshape(8, 32, N)
+            acc1[p, i] = (mine.astype(F32) + r1buf[p, i].astype(F32)).astype(BF)
+            return 0
+
+        lax.fori_loop(0, SEQ, one, 0)
+        for k in range(1, 8):
+            to_chip(p, k).start()
 
     def carried(k, _):
         @pl.when(k > 0)
@@ -309,7 +352,6 @@
         S = S_buf[i]
         mixed = dot(C, S) * lead + mix[:, cols].astype(F32)
         nb[:, cols] = (nb[:, cols].astype(F32) - mixed).astype(BF)
-        old_copy(i).start()
         gs = (gb[:, cols].astype(F32) * lead).astype(BF)
         dC[...] += dot_nt(gs, S)
         return 0
@@ -318,7 +360,9 @@
 
     dSl = (dS[...] * RN).astype(BF)
     low[:, N:] = (dC[...] + dot(dSl, B)).astype(BF)
+    product(1)
     dB[...] = dot_tn(dSl, C)
+    join(1)
 
     def carried_back(k, _):
         @pl.when(k > 0)
@@ -336,44 +380,10 @@
 
     lax.fori_loop(0, SEQ, carried_back, 0)
     low[:, :N] = dB[...].astype(BF)
-
-    def to_sib(i):
-        return pltpu.make_async_remote_copy(
-            part.at[i, :, 1 - core], r1buf.at[i], u1.at[i], v1.at[i],
-            device_id=(s, sib), device_id_type=MESH,
-        )
-
-    def product(i, _):
-        cols = pl.ds(pl.multiple_of(i * Q, Q), Q)
-        v = dot_tn(X[:, cols], low[...]).astype(BF)
-        part[pl.ds(i, 1)] = v.reshape(1, 8, 2, 32, 256)
-        to_sib(i).start()
-        return 0
-
-    lax.fori_loop(0, SEQ, product, 0)
-
-    def join(i, _):
-        to_sib(i).wait()
-        mine = part[pl.ds(i, 1), :, pl.ds(core, 1)].reshape(8, 32, 256)
-        acc1[i] = (mine.astype(F32) + r1buf[i].astype(F32)).astype(BF)
-        return 0
-
-    lax.fori_loop(0, SEQ, join, 0)
-
-    def to_chip(k):
-        return pltpu.make_async_remote_copy(
-            acc1.at[:, (chip + k) % 8], r2buf.at[k - 1], u2.at[k - 1], v2.at[k - 1],
-            device_id=(s, (f + 2 * k) % FS), device_id_type=MESH,
-        )
-
-    for k in range(1, 8):
-        to_chip(k).start()
+    product(0)
+    join(0)
 
     loads[3].wait()
-
-    def grad_copy(b):
-        rows = pl.ds(pl.multiple_of(b * 128, 128), 128)
-        return pltpu.make_async_copy(cb.at[rows], grad_hbm.at[rows], gsem.at[b])
 
     def normback(b, _):
         rows = pl.ds(pl.multiple_of(b * 128, 128), 128)
@@ -391,16 +401,16 @@
             cols = slice(i * Q, (i + 1) * Q)
             v = r * ng[:, cols] - back * xb[rows, cols].astype(F32)
             cb[rows, cols] = (cb[rows, cols].astype(F32) + v).astype(BF)
-        grad_copy(b).start()
-        return 0
-
-    lax.fori_loop(0, 4, normback, 0)
-
-    total = acc1[:, pl.ds(chip, 1)].reshape(8, 32, 256).astype(F32)
-    for k in range(1, 8):
-        to_chip(k).wait()
-        total += r2buf[k - 1].astype(F32)
-    acc2[...] = total.astype(BF)
+        return 0
+
+    lax.fori_loop(0, NB_1, normback, 0)
+
+    for p in (1, 0):
+        total = acc1[p, :, pl.ds(chip, 1)].reshape(8, 32, N).astype(F32)
+        for k in range(1, 8):
+            to_chip(p, k).wait()
+            total += r2buf[p, k - 1].astype(F32)
+        acc2[:, :, p * N : (p + 1) * N] = total.astype(BF)
 
     def to_seq(k):
         return pltpu.make_async_remote_copy(
@@ -410,12 +420,10 @@
 
     for k in range(1, 8):
         to_seq(k).start()
-    for c in sends:
-        c.wait_send()
-    for i in range(SEQ):
-        old_copy(i).wait()
-    for b in range(4):
-        grad_copy(b).wait()
+    lax.fori_loop(NB_1, 4, normback, 0)
+    for p in range(2):
+        for k in range(1, 8):
+            to_peer(p, k).wait_send()
     total = acc2[pl.ds(s, 1)].reshape(32, 256).astype(F32)
     for k in range(1, 8):
         to_seq(k).wait()
@@ -427,12 +435,13 @@
     return jax.ShapeDtypeStruct(dims, dtype)
 
 
-HEADS_1 = 12
-HEADS_2 = 24
+HEADS_1 = 8
+HEADS_2 = 22
+NB_1 = 2
 VM = pl.BlockSpec(memory_space=pltpu.VMEM)
 ANY = pl.BlockSpec(memory_space=pl.ANY)
 DMA = pltpu.SemaphoreType.DMA
-LIMIT = 60 << 20
+LIMIT = 52 << 20
 
 
 def shards(middle, newest, middle_cot, newest_cot, log_decay, weights, gain):
@@ -440,28 +449,29 @@
         return pltpu.VMEM(dims, dtype)
 
     scratch = [
-        vm(T, D), vm(T, D), vm(T, D), vm(T, D), vm(T, D), vm(D, 2 * N), vm(T, 1, dtype=F32),
+        vm(T, D), vm(T, D), vm(D, T), vm(T, D), vm(D, 2 * N), vm(T, 1, dtype=F32),
         vm(T, 2 * N), vm(SEQ, N, Q), vm(SEQ, N, Q), vm(SEQ, 8, Q, dtype=F32),
-        vm(T, 3 * H), vm(T, 2 * H), vm(T, 2 * H), vm(T, 2 * H), vm(H, T, dtype=F32),
+        vm(T, 3 * H), vm(T, 2 * H), vm(T, 2 * H), vm(T, 2 * H),
+        vm(H, T, dtype=F32), vm(H, T, dtype=F32), vm(H, T, dtype=F32),
         vm(T, T, dtype=F32), vm(T, T, dtype=F32), vm(T, D), vm(T, D),
         vm(SEQ, N, Q), vm(SEQ, N, Q), vm(SEQ, 8, Q, dtype=F32),
         vm(SEQ, N, Q), vm(SEQ, N, Q), vm(SEQ, N, Q), vm(SEQ, N, Q),
-        vm(T, N, dtype=F32), vm(T, N, dtype=F32), vm(T, 2 * N), vm(128, D, dtype=F32),
-        vm(8, 8, 2, 32, 256), vm(8, 8, 32, 256), vm(8, 8, 32, 256), vm(7, 8, 32, 256),
+        vm(T, N, dtype=F32), vm(T, N, dtype=F32), vm(T, 2 * N), vm(128, D, dtype=F32), vm(N, T, dtype=F32),
+        vm(2, 8, 8, 2, 32, N), vm(2, 8, 8, 32, N), vm(2, 8, 8, 32, N), vm(2, 7, 8, 32, N),
         vm(8, 32, 256), vm(7, 32, 256),
-        DMA((4,)), DMA((8,)), DMA((4,)), DMA((7,)), DMA((7,)), DMA((8,)), DMA((8,)),
-    ] + [DMA((8,))] * 10 + [DMA((8,)), DMA((8,))] + [DMA((7,))] * 4
+        DMA((4,)), DMA((2, 8)), DMA((2, 8)), DMA((2, 8)), DMA((2, 8)),
+    ] + [DMA((8,))] * 10 + [DMA((2, 8)), DMA((2, 8)), DMA((2, 7)), DMA((2, 7)), DMA((7,)), DMA((7,))]
     old, out, grad = pl.pallas_call(
         whole_step,
         name="step",
-        out_shape=[shape(T, D), shape(T, D), shape(32, 2 * N, dtype=F32)],
+        out_shape=[vm(T, D), vm(T, D), vm(32, 2 * N, dtype=F32)],
         in_specs=[pl.BlockSpec(memory_space=pltpu.SMEM)] + [ANY] * 4 + [VM] * 2,
-        out_specs=[ANY, ANY, VM],
+        out_specs=[VM, VM, VM],
         scratch_shapes=scratch,
         compiler_params=pltpu.CompilerParams(
             collective_id=0, has_side_effects=True, vmem_limit_bytes=LIMIT
         ),
-    )(gain, middle[0], newest[0], middle_cot[0], newest_cot[0], log_decay[0], weights)
+    )(gain, middle[0], newest[0], middle_cot[0], newest_cot[0], log_decay[0].T, weights)
     return old[None], out[None], grad
 
 

time: 116 us -> 101 us (0.87)
  the two profiles are of different devices: /device:TPU:0 before, /device:TPU:30 now
where the time goes in v3:
time: 101 us
  Pallas kernels  96 us (95%)
  local copies, waits for them, and re-layouts  4.64 us (5%)
    pallas_call x1, Pallas kernels, shards(): pl.pallas_call(whole_step, name='step', out_shape=[vm(T, D), vm(T, D), vm...  96 us
    unnamed x3, local copies, waits for them, and re-layouts  4.64 us

profile of v3, /device:TPU:30, one launch (start us, length us, event | category | flops | bytes accessed | tf_op | source)
XLA Modules:
  0.0 101.2 jit_solution(5226523663880280711)
XLA Ops:
  0.6 96.0 %step.1 = (bf16[512,4096]{1,0:T(8,128)(2,1)S(1)}, bf16[512,4096]{1,0:T(8,128)(2,1)S(1)}, f32[32,256]{1,0:T(8,128)S(1)}) custom-call(f32[32]{0:T(128)} %gain_ref.1, bf16[512,4096]{1,0:T(8,128)(2,1)} %bitcast.11, bf16[512,4096]{1,0:T(8,128)(2,1)} %bitcast.12, bf16[512,4096]{1,0:T(8,128)(2,1)} %bitcast.13, bf16[512,4096]{1,0:T(8,128)(2,1)} %bitcast.14, ...), custom_call_target="tpu_custom_call" | custom-call | tf_op jit(solution)/shard_map/step/pallas_call | solution.py:464
  96.6 2.0 %copy.13 = bf16[1,512,4096]{2,1,0:T(8,128)(2,1)} copy(bf16[1,512,4096]{2,1,0:T(8,128)(2,1)S(1)} %bitcast.10) | data formatting | bytes 8388608
  98.6 2.0 %copy.14 = bf16[1,512,4096]{2,1,0:T(8,128)(2,1)} copy(bf16[1,512,4096]{2,1,0:T(8,128)(2,1)S(1)} %bitcast.9) | data formatting | bytes 8388608
  100.6 0.6 copy.15

commit v4 on v3

--- a/solution.py
+++ b/solution.py
@@ -72,25 +72,31 @@
     s = lax.axis_index("seq")
     f = lax.axis_index("fsdp")
     core = f % 2
-    chip = f // 2
+    side_x = f // 8
+    other = (f + 8) % FS
+    y = (f // 2) % 4
     sib = f + 1 - 2 * core
 
     loads = []
     for k, (a, b) in enumerate(((x_hbm, xb), (g_hbm, gb), (new_hbm, nb), (cot_hbm, cb))):
-        c = pltpu.make_async_copy(a, b, lsem.at[k])
-        c.start()
-        loads.append(c)
+        loads.append(pltpu.make_async_copy(a, b, lsem.at[k]))
+    loads[0].start()
 
     barrier = pltpu.get_barrier_semaphore()
-    for k in range(1, 8):
-        pl.semaphore_signal(
-            barrier, inc=1, device_id=(s, (f + 2 * k) % FS), device_id_type=MESH
-        )
-        pl.semaphore_signal(
-            barrier, inc=1, device_id=((s + k) % SEQ, f), device_id_type=MESH
-        )
-    pl.semaphore_signal(barrier, inc=1, device_id=(s, sib), device_id_type=MESH)
-    pl.semaphore_wait(barrier, 15)
+    def along_y(j):
+        return side_x * 8 + (f % 8 + 2 * j) % 8
+
+    def greet(where):
+        pl.semaphore_signal(barrier, inc=1, device_id=where, device_id_type=MESH)
+
+    for j in range(1, 4):
+        greet((s, along_y(j)))
+    for k in range(1, SEQ):
+        greet(((s + k) % SEQ, f))
+        greet(((s + k) % SEQ, other))
+    greet((s, other))
+    greet((s, sib))
+    pl.semaphore_wait(barrier, 19)
 
     def slot(i):
         return W.at[pl.ds(pl.multiple_of(i * 256, 256), 256)]
@@ -98,23 +104,39 @@
     def half(ref, p):
         return ref.at[:, pl.ds(p * N, N)]
 
-    def to_peer(p, k):
+    def to_peer(p, m):
+        if m == 4:
+            a, b, to = w_ref, slot(f), other
+        elif m < 4:
+            a, b, to = w_ref, slot(f), along_y(m)
+        else:
+            a, b, to = slot(other), slot(other), along_y(m - 4)
         return pltpu.make_async_remote_copy(
-            half(w_ref, p), half(slot(f), p), ss.at[p, k], rs.at[p, k],
-            device_id=(s, (f + 2 * k) % FS), device_id_type=MESH,
+            half(a, p), half(b, p), ss.at[p, m], rs.at[p, m],
+            device_id=(s, to), device_id_type=MESH,
         )
 
-    def on(p, k):
-        at = slot((f + FS - 2 * k) % FS)
+    def on(p, m):
+        at = slot(((side_x + m // 4) % 2) * 8 + (f % 8 + 8 - 2 * (m % 4)) % 8)
         return pltpu.make_async_remote_copy(
-            half(w_ref if k == 0 else at, p), half(at, p), cs.at[p, k], cr.at[p, k],
+            half(w_ref if m == 0 else at, p), half(at, p), cs.at[p, m], cr.at[p, m],
             device_id=(s, sib), device_id_type=MESH,
         )
 
+    def first_sends(p):
+        for m in (4, 1, 2, 3):
+            to_peer(p, m).start()
+
+    def forward(p):
+        to_peer(p, 4).wait_recv()
+        for m in (5, 6, 7):
+            to_peer(p, m).start()
+        on(p, 4).start()
+
+    first_sends(0)
     for p in range(2):
-        for k in range(1, 8):
-            to_peer(p, k).start()
         on(p, 0).start()
+    loads[1].start()
     W[pl.ds(pl.multiple_of(f * 256, 256), 256), :] = w_ref[...]
 
     run_rows, feed_rows = decays(ld_ref[...])
@@ -133,6 +155,7 @@
     for i in range(8):
         dec[i] = dot(total, pick(3, 4 * i, 4))
 
+    forward(0)
     loads[0].wait()
 
     def norm(i, _):
@@ -144,11 +167,14 @@
         return 0
 
     lax.fori_loop(0, T // 32, norm, 0)
+    for k in range(1, 8):
+        to_peer(0, k).wait_send()
+    first_sends(1)
 
     def gathered(p):
-        for k in range(1, 8):
-            to_peer(p, k).wait_recv()
-            on(p, k).start()
+        for m in (1, 2, 3, 5, 6, 7):
+            to_peer(p, m).wait_recv()
+            on(p, m).start()
         for k in range(8):
             on(p, k).wait()
 
@@ -182,6 +208,7 @@
 
     gathered(0)
     side[...] = project(0)
+    forward(1)
 
     def make_a(k, _):
         i = (s + k) % SEQ
@@ -210,14 +237,11 @@
             c = (side[...] * leadT[pl.ds(h, 1), :]).astype(BF)
             g = gb[:, pl.ds(pl.multiple_of(h * N, N), N)]
             GT[i, :, q * N : (q + 1) * N] = dot(c, g).astype(BF)
-
-        @pl.when(k < SEQ)
-        def _():
-            to_g(k).start()
-
         return 0
 
     lax.fori_loop(1, SEQ + 1, make_g, 0)
+    loads[2].start()
+    loads[3].start()
     B = proj[:, :N]
     C = proj[:, N:]
     a_in[pl.ds(s, 1)] = AT[pl.ds(s, 1)]
@@ -280,10 +304,27 @@
 
         lax.fori_loop(1, SEQ, one, 0)
 
-    lax.fori_loop(0, HEADS_1, head, 0)
+    def then(first, second, base):
+        def one(k, _):
+            first(k).wait_send()
+            second(k).start()
+            head(base + k - 1, 0)
+            return 0
+
+        lax.fori_loop(1, SEQ, one, 0)
+
+    def wait_recv(make):
+        def one(k, _):
+            make(k).wait_recv()
+            return 0
+
+        lax.fori_loop(1, SEQ, one, 0)
+
+    then(to_a, to_g, 0)
+    lax.fori_loop(SEQ - 1, HEADS_1, head, 0)
 
     wait_in(to_dec)
-    wait_in(to_a)
+    wait_recv(to_a)
     state = jnp.zeros((N, Q), F32)
     for j in range(SEQ):
         a_out[j] = state.astype(BF)
@@ -300,10 +341,10 @@
         g_out[j] = state.astype(BF)
         if j > 0:
             state = d_in[j, 0:1, :] * state + g_in[j].astype(F32)
-    start_back(back_g)
+    then(back_a, back_g, HEADS_2)
     G_buf[pl.ds(s, 1)] = g_out[pl.ds(s, 1)]
 
-    lax.fori_loop(HEADS_2, H, head, 0)
+    lax.fori_loop(HEADS_2 + SEQ - 1, H, head, 0)
     loads[2].wait()
 
     def to_sib(p, i):
@@ -312,10 +353,10 @@
             device_id=(s, sib), device_id_type=MESH,
         )
 
-    def to_chip(p, k):
+    def to_y(p, j):
         return pltpu.make_async_remote_copy(
-            acc1.at[p, :, (chip + k) % 8], r2buf.at[p, k - 1], u2.at[p, k - 1], v2.at[p, k - 1],
-            device_id=(s, (f + 2 * k) % FS), device_id_type=MESH,
+            acc1.at[p, :, :, (y + j) % 4], r2buf.at[p, j - 1], u2.at[p, j - 1], v2.at[p, j - 1],
+            device_id=(s, along_y(j)), device_id_type=MESH,
         )
 
     def product(p):
@@ -334,17 +375,18 @@
         def one(i, _):
             to_sib(p, i).wait()
             mine = part[p, pl.ds(i, 1), :, pl.ds(core, 1)].reshape(8, 32, N)
-            acc1[p, i] = (mine.astype(F32) + r1buf[p, i].astype(F32)).astype(BF)
+            v = (mine.astype(F32) + r1buf[p, i].astype(F32)).astype(BF)
+            acc1[p, i] = v.reshape(2, 4, 32, N)
             return 0
 
         lax.fori_loop(0, SEQ, one, 0)
-        for k in range(1, 8):
-            to_chip(p, k).start()
+        for j in range(1, 4):
+            to_y(p, j).start()
 
     def carried(k, _):
         @pl.when(k > 0)
         def _():
-            back_a(k).wait()
+            back_a(k).wait_recv()
 
         i = (s + SEQ - k) % SEQ
         cols = pl.ds(pl.multiple_of(i * Q, Q), Q)
@@ -406,36 +448,49 @@
     lax.fori_loop(0, NB_1, normback, 0)
 
     for p in (1, 0):
-        total = acc1[p, :, pl.ds(chip, 1)].reshape(8, 32, N).astype(F32)
-        for k in range(1, 8):
-            to_chip(p, k).wait()
-            total += r2buf[p, k - 1].astype(F32)
-        acc2[:, :, p * N : (p + 1) * N] = total.astype(BF)
-
-    def to_seq(k):
+        total = acc1[p, :, :, pl.ds(y, 1)].reshape(8, 2, 32, N).astype(F32)
+        for j in range(1, 4):
+            to_y(p, j).wait()
+            total += r2buf[p, j - 1].astype(F32)
+        acc2[:, :, :, p * N : (p + 1) * N] = total.astype(BF)
+
+    def to_end(m):
+        place, row = (side_x + m // 8) % 2, (s + m % 8) % SEQ
         return pltpu.make_async_remote_copy(
-            acc2.at[(s + k) % SEQ], r3buf.at[k - 1], u3.at[k - 1], v3.at[k - 1],
-            device_id=((s + k) % SEQ, f), device_id_type=MESH,
+            acc2.at[row, place], r3buf.at[m - 1], u3.at[m - 1], v3.at[m - 1],
+            device_id=(row, place * 8 + f % 8), device_id_type=MESH,
         )
 
+    for m in range(1, 16):
+        to_end(m).start()
+    lax.fori_loop(NB_1, 4, normback, 0)
     for k in range(1, 8):
-        to_seq(k).start()
-    lax.fori_loop(NB_1, 4, normback, 0)
-    for p in range(2):
-        for k in range(1, 8):
-            to_peer(p, k).wait_send()
-    total = acc2[pl.ds(s, 1)].reshape(32, 256).astype(F32)
-    for k in range(1, 8):
-        to_seq(k).wait()
-        total += r3buf[k - 1].astype(F32)
+        to_peer(1, k).wait_send()
+    total = acc2[pl.ds(s, 1), pl.ds(side_x, 1)].reshape(32, 256).astype(F32)
+    for m in range(1, 16):
+        to_end(m).wait()
+        total += r3buf[m - 1].astype(F32)
     dw_ref[...] = total * (T * SEQ * FS) ** (-0.5)
+
+
+def store(old_ref, grad_ref, dw_ref, old_hbm, grad_hbm, dw_hbm, sem):
+    copies = []
+    for p in range(4):
+        rows = pl.ds(p * 128, 128)
+        for n, (a, b) in enumerate(((old_ref, old_hbm), (grad_ref, grad_hbm))):
+            copies.append(pltpu.make_async_copy(a.at[rows], b.at[rows], sem.at[2 * p + n]))
+    copies.append(pltpu.make_async_copy(dw_ref, dw_hbm, sem.at[8]))
+    for c in copies:
+        c.start()
+    for c in copies:
+        c.wait()
 
 
 def shape(*dims, dtype=BF):
     return jax.ShapeDtypeStruct(dims, dtype)
 
 
-HEADS_1 = 8
+HEADS_1 = 9
 HEADS_2 = 22
 NB_1 = 2
 VM = pl.BlockSpec(memory_space=pltpu.VMEM)
@@ -457,10 +512,10 @@
         vm(SEQ, N, Q), vm(SEQ, N, Q), vm(SEQ, 8, Q, dtype=F32),
         vm(SEQ, N, Q), vm(SEQ, N, Q), vm(SEQ, N, Q), vm(SEQ, N, Q),
         vm(T, N, dtype=F32), vm(T, N, dtype=F32), vm(T, 2 * N), vm(128, D, dtype=F32), vm(N, T, dtype=F32),
-        vm(2, 8, 8, 2, 32, N), vm(2, 8, 8, 32, N), vm(2, 8, 8, 32, N), vm(2, 7, 8, 32, N),
-        vm(8, 32, 256), vm(7, 32, 256),
+        vm(2, 8, 8, 2, 32, N), vm(2, 8, 8, 32, N), vm(2, 8, 2, 4, 32, N), vm(2, 3, 8, 2, 32, N),
+        vm(8, 2, 32, 256), vm(15, 32, 256),
         DMA((4,)), DMA((2, 8)), DMA((2, 8)), DMA((2, 8)), DMA((2, 8)),
-    ] + [DMA((8,))] * 10 + [DMA((2, 8)), DMA((2, 8)), DMA((2, 7)), DMA((2, 7)), DMA((7,)), DMA((7,))]
+    ] + [DMA((8,))] * 10 + [DMA((2, 8)), DMA((2, 8)), DMA((2, 3)), DMA((2, 3)), DMA((15,)), DMA((15,))]
     old, out, grad = pl.pallas_call(
         whole_step,
         name="step",
@@ -472,6 +527,16 @@
             collective_id=0, has_side_effects=True, vmem_limit_bytes=LIMIT
         ),
     )(gain, middle[0], newest[0], middle_cot[0], newest_cot[0], log_decay[0].T, weights)
+    held = [pltpu.with_memory_space_constraint(a, pltpu.VMEM) for a in (old, out, grad)]
+    old, out, grad = pl.pallas_call(
+        store,
+        name="store",
+        out_shape=[shape(T, D), shape(T, D), shape(32, 2 * N, dtype=F32)],
+        in_specs=[VM] * 3,
+        out_specs=[ANY] * 3,
+        scratch_shapes=[DMA((9,))],
+        compiler_params=pltpu.CompilerParams(vmem_limit_bytes=4 << 20),
+    )(*held)
     return old[None], out[None], grad
 
 

time: 101 us -> 98.9 us (0.979)
  the two profiles are of different devices: /device:TPU:30 before, /device:TPU:0 now
where the time goes in v4:
time: 98.9 us; the launch traced here: 98.8 us
  Pallas kernels  98.1 us (99%)
    pallas_call x1, Pallas kernels, shards(): pl.pallas_call(whole_step, name='step', out_shape=[vm(T, D), vm(T, D), vm...  94.8 us
    pallas_call x1, Pallas kernels, shards(): pl.pallas_call(store, name='store', out_shape=[shape(T, D), shape(T, D),...  3.38 us

profile of v4, /device:TPU:0, one launch (start us, length us, event | category | flops | bytes accessed | tf_op | source)
XLA Modules:
  0.0 98.8 jit_solution(2898905234469117342)
XLA Ops:
  0.6 94.8 %step.1 = (bf16[512,4096]{1,0:T(8,128)(2,1)S(1)}, bf16[512,4096]{1,0:T(8,128)(2,1)S(1)}, f32[32,256]{1,0:T(8,128)S(1)}) custom-call(f32[32]{0:T(128)} %gain_ref.1, bf16[512,4096]{1,0:T(8,128)(2,1)} %bitcast.9, bf16[512,4096]{1,0:T(8,128)(2,1)} %bitcast.10, bf16[512,4096]{1,0:T(8,128)(2,1)} %bitcast.11, bf16[512,4096]{1,0:T(8,128)(2,1)} %bitcast.12, ...), custom_call_target="tpu_custom_call" | custom-call | tf_op jit(solution)/shard_map/step/pallas_call | solution.py:519
  95.4 3.4 %store.1 = (bf16[512,4096]{1,0:T(8,128)(2,1)}, bf16[512,4096]{1,0:T(8,128)(2,1)}, f32[32,256]{1,0:T(8,128)}) custom-call(bf16[512,4096]{1,0:T(8,128)(2,1)S(1)} %get-tuple-element.9.old_ref, bf16[512,4096]{1,0:T(8,128)(2,1)S(1)} %get-tuple-element.10.grad_ref, f32[32,256]{1,0:T(8,128)S(1)} %get-tuple-element.11.dw_ref), custom_call_target="tpu_custom_call" | custom-call | tf_op jit(solution)/shard_map/store/pallas_call | solution.py:531

commit v5 on v4

--- a/solution.py
+++ b/solution.py
@@ -491,7 +491,7 @@
 
 
 HEADS_1 = 9
-HEADS_2 = 22
+HEADS_2 = 25
 NB_1 = 2
 VM = pl.BlockSpec(memory_space=pltpu.VMEM)
 ANY = pl.BlockSpec(memory_space=pl.ANY)

time: 98.9 us -> 97.5 us (0.986)
  Pallas kernels: 98.1 us -> 96.7 us
    pallas_call x1, Pallas kernels: 94.8 us -> 93.3 us  [shards(): pl.pallas_call(whole_step, name='step', out_shape=[vm(T, D), vm(T, D), vm...]
where the time goes in v5:
time: 97.5 us; the launch traced here: 97.4 us
  Pallas kernels  96.7 us (99%)
    pallas_call x1, Pallas kernels, shards(): pl.pallas_call(whole_step, name='step', out_shape=[vm(T, D), vm(T, D), vm...  93.3 us
    pallas_call x1, Pallas kernels, shards(): pl.pallas_call(store, name='store', out_shape=[shape(T, D), shape(T, D),...  3.38 us

profile of v5, /device:TPU:0, one launch (start us, length us, event | category | flops | bytes accessed | tf_op | source)
XLA Modules:
  0.0 97.4 jit_solution(807800417570337632)
XLA Ops:
  0.6 93.3 %step.1 = (bf16[512,4096]{1,0:T(8,128)(2,1)S(1)}, bf16[512,4096]{1,0:T(8,128)(2,1)S(1)}, f32[32,256]{1,0:T(8,128)S(1)}) custom-call(f32[32]{0:T(128)} %gain_ref.1, bf16[512,4096]{1,0:T(8,128)(2,1)} %bitcast.9, bf16[512,4096]{1,0:T(8,128)(2,1)} %bitcast.10, bf16[512,4096]{1,0:T(8,128)(2,1)} %bitcast.11, bf16[512,4096]{1,0:T(8,128)(2,1)} %bitcast.12, ...), custom_call_target="tpu_custom_call" | custom-call | tf_op jit(solution)/shard_map/step/pallas_call | solution.py:519
  94.0 3.4 %store.1 = (bf16[512,4096]{1,0:T(8,128)(2,1)}, bf16[512,4096]{1,0:T(8,128)(2,1)}, f32[32,256]{1,0:T(8,128)}) custom-call(bf16[512,4096]{1,0:T(8,128)(2,1)S(1)} %get-tuple-element.9.old_ref, bf16[512,4096]{1,0:T(8,128)(2,1)S(1)} %get-tuple-element.10.grad_ref, f32[32,256]{1,0:T(8,128)S(1)} %get-tuple-element.11.dw_ref), custom_call_target="tpu_custom_call" | custom-call | tf_op jit(solution)/shard_map/store/pallas_call | solution.py:531
